TPU v7x, 128 devices: a whole 4x4x4 slice. The times are simulated.
128 devices in a mesh: dom: 128 (over y, x, z, core).
Axes of the slice: x: 4, y: 4, z: 4, core: 2. Of those that a mesh axis runs over, the one named last changes fastest.
Arguments:
- disp: float32 [3, 524288], P(None, 'dom'), may hold values from -6 to 6
- direction: float32 [3, 524288], P(None, 'dom'), may hold values from -6 to 6
- load: float32 [3, 524288], P(None, 'dom'), may hold values from -6 to 6
- blocks: bfloat16 [96, 96, 65536], P(None, None, 'dom'), may hold values from -0.625 to 0.625
- elem_nodes: int32 [32, 65536], P(None, 'dom'), may hold values from 0 to 5119
- halo_send: int32 [512, 256], P('dom'), may hold values from 0 to 4095
- master_nodes: int32 [16384, 12], P('dom'), may hold values from 0 to 4095
- slave_nodes: int32 [16384, 12], P('dom'), may hold values from 0 to 4095
- mortar_send: int32 [128, 128, 32], P('dom'), may hold values from 0 to 127
- mortar_count: int32 [128, 128], P('dom'), may hold values from 0 to 32, as said below
- pair_slave: int32 [524288], P('dom'), may hold values from 0 to 127
- slave_mortar: float32 [9, 36, 524288], P(None, None, 'dom'), may hold values from -1.2 to 1.2
- master_mortar: float32 [9, 36, 524288], P(None, None, 'dom'), may hold values from -1.2 to 1.2
- gap_offset: float32 [9, 524288], P(None, 'dom'), may hold values from -6 to 6
Outputs:
- residual: float32 [3, 524288], P(None, 'dom')
- applied: float32 [3, 524288], P(None, 'dom')
Inputs may be any that keep to these rules, and one draw needn't show every extreme that they name: `mortar_count`: at most 32 live slots from one partition to one peer; every partition fills all 32 slots to at least one peer.
All inputs are finite; a program needn't handle non-finite values.
Results may differ from a plain program's by a relative error of at most 0.0012.
Values may be sent and summed in bfloat16 or wider, within the bound.
No kernel may reach another device: no remote copies, remote signals or barrier semaphores. Data moves between devices by JAX's collectives and lax.ppermute only.
A program may use at most 128 MiB of HBM per device.

v0:
```python
import jax
import jax.numpy as jnp
from jax import lax
from jax.sharding import PartitionSpec as P

REACH = 2


def shifted(value, axis, steps):
    count = lax.axis_size(axis)
    pairs = [(source, (source + steps) % count) for source in range(count)]
    return lax.ppermute(value, axis, pairs)


def offsets():
    return [move for move in range(-REACH, REACH + 1) if move != 0]


def apply_block(matrix, vector):
    return jnp.einsum("qkp,kp->qp", matrix, vector, precision=lax.Precision.HIGHEST)


def adjoint_block(matrix, vector):
    return jnp.einsum("qkp,qp->kp", matrix, vector, precision=lax.Precision.HIGHEST)


def select_columns(source, positions):
    row_count, col_count = source.shape
    groups = -(-col_count // 128)
    padded = source.reshape(row_count * groups, 128)
    flat_index = positions.reshape(-1)
    lane_hits = (jnp.arange(128, dtype=jnp.int32)[:, None] == (flat_index % 128)[None, :]).astype(
        source.dtype
    )
    widened = jnp.dot(
        padded, lane_hits, preferred_element_type=jnp.float32, precision=lax.Precision.HIGHEST
    )
    widened = widened.reshape(row_count, groups, flat_index.shape[0])
    group_hits = jnp.arange(groups, dtype=jnp.int32)[:, None] == (flat_index // 128)[None, :]
    result = jnp.sum(jnp.where(group_hits[None], widened, 0.0), axis=1).astype(source.dtype)
    return result.reshape((row_count,) + positions.shape)


def spread_columns(values, positions, col_count):
    row_count = values.shape[0]
    groups = -(-col_count // 128)
    flat_index = positions.reshape(-1)
    flat_values = values.reshape(row_count, -1)
    group_hits = jnp.arange(groups, dtype=jnp.int32)[:, None] == (flat_index // 128)[None, :]
    widened = jnp.where(group_hits[None], flat_values[:, None, :], 0.0).reshape(
        row_count * groups, -1
    )
    lane_hits = ((flat_index % 128)[:, None] == jnp.arange(128, dtype=jnp.int32)[None, :]).astype(
        jnp.float32
    )
    placed = jnp.dot(
        widened, lane_hits, preferred_element_type=jnp.float32, precision=lax.Precision.HIGHEST
    )
    return placed.reshape(row_count, groups * 128)


def device_work(
    extended,
    fields,
    blocks,
    elem_nodes,
    slave_nodes,
    pair_slave,
    slave_mortar,
    master_mortar,
    gap_offset,
    remote,
    live,
):
    elements = blocks.shape[2]
    ext_count = extended.shape[1]
    own_count = fields.shape[1]
    picked = select_columns(extended, elem_nodes).reshape(2, 96, elements)
    forces = jnp.einsum("ije,wje->wie", blocks, picked, preferred_element_type=jnp.float32)
    forces = forces.reshape(6, 32, elements)
    totals = spread_columns(forces, elem_nodes, ext_count)
    slave_index = slave_nodes[pair_slave]
    nearby = select_columns(fields, slave_index).transpose(0, 2, 1).reshape(72, -1)
    opening = (
        apply_block(slave_mortar, nearby[:36])
        + apply_block(master_mortar, remote[:36])
        + gap_offset
    )
    tangent = apply_block(slave_mortar, nearby[36:]) + apply_block(master_mortar, remote[36:])
    pressure = jax.nn.softplus(opening) * live
    increment = jax.nn.sigmoid(opening) * tangent * live
    slave_force = jnp.concatenate(
        [adjoint_block(slave_mortar, pressure), adjoint_block(slave_mortar, increment)], 0
    )
    master_force = jnp.concatenate(
        [adjoint_block(master_mortar, pressure), adjoint_block(master_mortar, increment)], 0
    )
    contact = spread_columns(slave_force.reshape(6, 12, -1), slave_index.T, own_count)
    totals = jnp.concatenate([totals[:, :own_count] + contact, totals[:, own_count:]], axis=1)
    return (totals, master_force)


def on_device(
    disp,
    direction,
    load,
    blocks,
    elem_nodes,
    halo_send,
    master_nodes,
    slave_nodes,
    mortar_send,
    mortar_count,
    pair_slave,
    slave_mortar,
    master_mortar,
    gap_offset,
):
    peers = lax.axis_size("dom")
    own_rows = disp.shape[1]
    moves = offsets()
    width = halo_send.shape[1]
    fields = jnp.concatenate([disp, direction], 0)
    coarse = fields.astype(jnp.bfloat16)
    outgoing = select_columns(coarse, halo_send)
    pieces = [shifted(outgoing[:, slot], "dom", moves[slot]) for slot in range(len(moves))]
    extended = jnp.concatenate([coarse] + pieces, axis=1)
    master_index = master_nodes[mortar_send[0]]
    master_values = (
        select_columns(fields, master_index).transpose(0, 3, 1, 2).reshape(72, peers, -1)
    )
    slots = master_values.shape[2]
    live_slots = (jnp.arange(slots, dtype=jnp.int32)[None, :] < mortar_count[0][:, None]).astype(
        jnp.float32
    )[None]
    remote, live = (
        lax.all_to_all(master_values, "dom", split_axis=1, concat_axis=1, tiled=True),
        lax.all_to_all(live_slots, "dom", split_axis=1, concat_axis=1, tiled=True),
    )
    totals, master_force = device_work(
        extended,
        fields,
        blocks,
        elem_nodes,
        slave_nodes,
        pair_slave,
        slave_mortar,
        master_mortar,
        gap_offset,
        remote.reshape(72, peers * slots),
        live.reshape(1, peers * slots),
    )
    owned = totals[:, :own_rows]
    sums = totals[:, own_rows:].reshape(6, len(moves), width)
    returned_force = lax.all_to_all(
        master_force.reshape(72, peers, slots), "dom", split_axis=1, concat_axis=1, tiled=True
    )
    shared = [shifted(sums[:, slot], "dom", -moves[slot]) for slot in range(len(moves))]
    stacked = jnp.stack(shared, axis=1)
    owned = owned + spread_columns(stacked, halo_send, own_rows)
    owned = owned + spread_columns(
        returned_force.reshape(6, 12, peers, slots), master_index.transpose(2, 0, 1), own_rows
    )
    return (load - owned[:3], owned[3:])


def solution(mesh):
    return jax.shard_map(
        on_device,
        mesh=mesh,
        in_specs=(
            P(None, "dom"),
            P(None, "dom"),
            P(None, "dom"),
            P(None, None, "dom"),
            P(None, "dom"),
            P("dom", None),
            P("dom", None),
            P("dom", None),
            P("dom", None, None),
            P("dom", None),
            P("dom"),
            P(None, None, "dom"),
            P(None, None, "dom"),
            P(None, "dom"),
        ),
        out_specs=(P(None, "dom"), P(None, "dom")),
        check_vma=False,
    )
```

profile of v0, /device:TPU:0, one launch (start us, length us, event | category | flops | bytes accessed | tf_op | source)
XLA Modules:
  0.0 415.9 jit_solution(12815341694369005657)
XLA Ops:
  0.6 1.5 compare_convert_fusion
  2.1 11.1 %all-to-all-start.1 = ((f32[1,128,32]{2,0,1:T(1,128)}), f32[1,128,32]{2,0,1:T(1,128)S(1)}, u32[]{:S(2)}, u32[]{:S(2)}) async-start(f32[1,128,32]{2,0,1:T(1,128)} %compare_convert_fusion), calls=%async_computation.1 | async-start | bytes 131072 | tf_op jit(solution)/shard_map/all_to_all | solution.py:138
  15.9 7.3 %collective-permute-start = (bf16[6,256]{1,0:T(8,128)(2,1)}, bf16[6,256]{1,0:T(8,128)(2,1)}, u32[]{:S(2)}, u32[]{:S(2)}) collective-permute-start(bf16[6,256]{1,0:T(8,128)(2,1)} %get-tuple-element.36), channel_id=1, source_target_pairs={{0,126},{1,127},{2,0},{3,1},{4,2},{5,3},{6,4},{7,5},{8,6},{9,7},{1... | collective-permute-start | bytes 9224 | tf_op jit(solution)/shard_map/ppermute | solution.py:12
  23.7 1.2 collective-permute-start.3
  27.3 10.8 %gather_fusion.1 = s32[4096,12]{1,0:T(8,128)S(1)} fusion(s32[128,12]{1,0:T(8,128)S(1)} %copy.64, s32[4096]{0:T(1024)S(1)} %get-tuple-element.40), kind=kCustom, calls=%fused_computation.1 | custom fusion | bytes 409600 | tf_op jit(solution)/shard_map/gather | solution.py:128
  38.1 1.9 reshape.633
  40.9 2.0 iota_compare_fusion.10
  42.9 14.1 %gather_fusion = s32[4096,12]{1,0:T(8,128)} fusion(s32[128,12]{1,0:T(8,128)S(1)} %copy.60, s32[4096]{0:T(1024)S(1)} %get-tuple-element.39), kind=kCustom, calls=%fused_computation | custom fusion | bytes 409600 | tf_op jit(solution)/shard_map/gather | solution.py:82
  57.0 3.4 reshape.631
  61.5 20.3 %fusion.13 = f32[6,49152]{1,0:T(8,128)} fusion(s32[49152]{0:T(1024)S(1)} %get-tuple-element.25, pred[32,49152]{1,0:T(8,128)(4,1)S(1)} %iota_compare_fusion.11, f32[1,6,32,128]{3,1,2,0:T(8,128)S(1)} %fusion.44), kind=kOutput, calls=%fused_computation.28 | convolution fusion | flops 14520385536 | bytes 3047424 | tf_op jit(solution)/shard_map/dot_general | solution.py:35
  81.8 19.8 %reshape.632 = f32[6,4096,12]{2,1,0:T(8,128)} reshape(f32[6,49152]{1,0:T(8,128)} %fusion.13) | data formatting | bytes 2359296 | tf_op jit(solution)/shard_map/reshape | solution.py:41
  101.6 10.0 %fusion.58 = (f32[3,12,4096]{1,2,0:T(8,128)}, f32[3,12,4096]{1,2,0:T(8,128)}) fusion(f32[6,12,4096]{1,2,0:T(8,128)} %bitcast.138), kind=kLoop, calls=%fused_computation.143 | loop fusion | bytes 2359296 | tf_op jit(solution)/shard_map/slice | solution.py:89
  111.6 2.2 copy.61
  114.7 2.0 iota_compare_fusion.12
  116.7 1.0 copy.73
  118.8 2.0 iota_compare_fusion.9
  121.2 20.4 %fusion.16 = f32[6,49152]{1,0:T(8,128)S(1)} fusion(s32[49152]{0:T(1024)} %get-tuple-element.23, pred[32,49152]{1,0:T(8,128)(4,1)} %iota_compare_fusion.10, f32[1,6,32,128]{3,1,2,0:T(8,128)} %copy-done.11), kind=kOutput, calls=%fused_computation.29 | convolution fusion | flops 14520385536 | bytes 3047424 | tf_op jit(solution)/shard_map/dot_general | solution.py:35
  142.3 18.4 %reshape.634 = f32[6,128,32,12]{3,2,1,0:T(8,128)} reshape(f32[6,49152]{1,0:T(8,128)S(1)} %fusion.16) | data formatting | bytes 2359296 | tf_op jit(solution)/shard_map/reshape | solution.py:41
  160.7 9.4 %copy.65 = f32[6,12,128,32]{2,3,1,0:T(8,128)S(1)} copy(f32[6,12,128,32]{1,3,2,0:T(8,128)} %bitcast.139) | data formatting | bytes 2359296 | tf_op jit(solution)/shard_map/transpose | solution.py:130
  170.1 2.1 copy.66
  172.2 4.4 %copy.62 = f32[3,12,4096]{2,1,0:T(8,128)S(1)} copy(f32[3,12,4096]{1,2,0:T(8,128)} %get-tuple-element.13) | data formatting | bytes 1179648 | tf_op jit(solution)/shard_map/slice | solution.py:85
  176.7 4.4 %copy.68 = f32[3,12,4096]{2,1,0:T(8,128)S(1)} copy(f32[3,12,4096]{1,2,0:T(8,128)} %get-tuple-element.12) | data formatting | bytes 1179648 | tf_op jit(solution)/shard_map/slice | solution.py:89
  181.2 16.0 %copy.58 = bf16[96,96,512]{1,0,2:T(8,128)(2,1)} copy(bf16[96,96,512]{2,1,0:T(8,128)(2,1)} %param.17) | data formatting | bytes 18874368 | tf_op args[3]
  198.0 4.3 %fusion.21 = bf16[6,16384]{1,0:T(8,128)(2,1)S(1)} fusion(s32[16384]{0:T(1024)S(1)} %get-tuple-element.29, pred[40,16384]{1,0:T(8,128)(4,1)S(1)} %iota_compare_fusion.13, bf16[1,6,40,128]{3,1,2,0:T(8,128)(2,1)S(1)} %bitcast.159), kind=kOutput, calls=%fused_computation.40 | convolution fusion | flops 1016496128 | bytes 978944 | tf_op jit(solution)/shard_map/dot_general | solution.py:35
  202.7 9.5 %convolution_bitcast_fusion = f32[2,96,512]{1,0,2:T(2,128)S(1)} fusion(bf16[2,96,512]{1,0,2:T(2,128)(2,1)S(1)} %copy.57, bf16[96,96,512]{1,0,2:T(8,128)(2,1)} %copy.58), kind=kOutput, calls=%fused_computation.44 | convolution fusion | flops 18874368 | bytes 10027008 | tf_op jit(solution)/shard_map/ije,wje->wie/dot_general | solution.py:79
  212.6 7.2 %broadcast_select_fusion.2 = f32[6,40,16384]{2,1,0:T(8,128)} fusion(f32[6,16384]{1,0:T(8,128)S(1)} %broadcast_in_dim.161, pred[40,16384]{1,0:T(8,128)(4,1)S(1)} %iota_compare_fusion.13), kind=kLoop, calls=%fused_computation.23 | loop fusion | flops 3932160 | bytes 16777216 | tf_op jit(solution)/shard_map/jit(_where)/select_n | solution.py:50
  219.8 13.5 %fusion.12 = f32[240,128]{1,0:T(8,128)S(1)} fusion(f32[240,16384]{1,0:T(8,128)} %bitcast.137, s32[16384]{0:T(1024)S(1)} %get-tuple-element.29), kind=kOutput, calls=%fused_computation.22 | convolution fusion | flops 6041894912 | bytes 15917056 | tf_op jit(solution)/shard_map/dot_general | solution.py:56
  234.1 8.8 %all-to-all-start = ((f32[72,128,32]{0,2,1:T(8,128)}), f32[72,128,32]{0,2,1:T(8,128)S(1)}, u32[]{:S(2)}, u32[]{:S(2)}) async-start(f32[72,128,32]{0,2,1:T(8,128)} %copy.66), calls=%async_computation | async-start | bytes 4194304 | tf_op jit(solution)/shard_map/all_to_all | solution.py:137
  242.9 1.1 collective-permute-start.4
  244.1 7.2 %collective-permute-start.6 = (f32[6,256]{1,0:T(8,128)S(1)}, f32[6,256]{1,0:T(8,128)S(1)}, u32[]{:S(2)}, u32[]{:S(2)}) collective-permute-start(f32[6,256]{1,0:T(8,128)S(1)} %get-tuple-element.31), channel_id=1, source_target_pairs={{0,127},{1,0},{2,1},{3,2},{4,3},{5,4},{6,5},{7,6},{8,7},{9,8},{10,... | collective-permute-start | bytes 18440 | tf_op jit(solution)/shard_map/ppermute | solution.py:12
  252.0 1.2 collective-permute-start.7
  253.2 4.9 %multiply_reduce_fusion.7 = (f32[4096,9]{0,1:T(8,128)}, f32[4096,9]{0,1:T(8,128)}) fusion(f32[9,36,4096]{2,1,0:T(8,128)} %param.25, f32[4096,36]{0,1:T(8,128)S(1)} %bitcast.153, f32[4096,36]{0,1:T(8,128)S(1)} %bitcast.154), kind=kLoop, calls=%fused_computation.37 | loop fusion | flops 5234688 | bytes 6782976 | tf_op jit(solution)/shard_map/qkp,kp->qp/dot_general | solution.py:20
  258.1 15.0 %collective-permute-done.4 = f32[6,256]{1,0:T(8,128)S(1)} collective-permute-done((f32[6,256]{1,0:T(8,128)S(1)}, f32[6,256]{1,0:T(8,128)S(1)}, u32[]{:S(2)}, u32[]{:S(2)}) %collective-permute-start.4) | collective-permute-done | bytes 6176 | tf_op jit(solution)/shard_map/ppermute | solution.py:12
  276.0 2.7 fusion.59
  278.7 2.2 copy.131
  281.0 2.4 copy.134
  283.4 4.3 %multiply_reduce_fusion.6 = (f32[4096,9]{0,1:T(8,128)S(1)}, f32[4096,9]{0,1:T(8,128)S(1)}) fusion(f32[9,36,4096]{2,1,0:T(8,128)} %param.26, f32[4096,36]{0,1:T(8,128)S(1)} %copy.131, f32[4096,36]{0,1:T(8,128)S(1)} %copy.134), kind=kLoop, calls=%fused_computation.36 | loop fusion | flops 5234688 | bytes 6782976 | tf_op jit(solution)/shard_map/qkp,kp->qp/dot_general | solution.py:20
  287.9 4.0 multiply_reduce_fusion.1
  292.0 1.7 broadcast_in_dim.168
  294.4 2.1 copy.124
  296.5 3.5 pad_maximum_fusion
  300.0 4.9 %all-to-all-start.2 = ((f32[72,128,32]{0,2,1:T(8,128)}), f32[72,128,32]{0,2,1:T(8,128)S(1)}, u32[]{:S(2)}, u32[]{:S(2)}) async-start(f32[72,128,32]{0,2,1:T(8,128)} %bitcast.58), calls=%async_computation.2 | async-start | bytes 4194304 | tf_op jit(solution)/shard_map/all_to_all | solution.py:155
  304.9 5.3 %broadcast_select_fusion.1 = f32[6,32,49152]{2,1,0:T(8,128)S(1)} fusion(f32[6,49152]{1,0:T(8,128)} %broadcast_in_dim.168, pred[32,49152]{1,0:T(8,128)(4,1)} %iota_compare_fusion.12), kind=kLoop, calls=%fused_computation.14 | loop fusion | flops 9437184 | bytes 40501248 | tf_op jit(solution)/shard_map/jit(_where)/select_n | solution.py:50
  310.2 46.0 %fusion.4 = f32[192,128]{1,0:T(8,128)S(1)} fusion(f32[192,49152]{1,0:T(8,128)S(1)} %bitcast.135, s32[49152]{0:T(1024)S(1)} %copy-done.2), kind=kOutput, calls=%fused_computation.10 | convolution fusion | flops 14501806080 | bytes 38043648 | tf_op jit(solution)/shard_map/dot_general | solution.py:56
  356.3 3.9 copy.74
  360.2 4.4 %broadcast_in_dim.173 = f32[6,49152]{1,0:T(8,128)S(1)} reshape(f32[72,128,32]{2,1,0:T(8,128)} %copy.74) | data formatting | bytes 2359296 | tf_op jit(solution)/shard_map/jit(_where)/broadcast_in_dim | solution.py:50
  364.5 4.2 %broadcast_select_fusion = f32[6,32,49152]{2,1,0:T(8,128)S(1)} fusion(f32[6,49152]{1,0:T(8,128)S(1)} %broadcast_in_dim.173, pred[32,49152]{1,0:T(8,128)(4,1)S(1)} %copy-done), kind=kLoop, calls=%fused_computation.13 | loop fusion | flops 9437184 | bytes 40501248 | tf_op jit(solution)/shard_map/jit(_where)/select_n | solution.py:50
  368.8 46.0 %fusion.5 = f32[192,128]{1,0:T(8,128)S(1)} fusion(f32[192,49152]{1,0:T(8,128)S(1)} %bitcast.136, s32[49152]{0:T(1024)S(1)} %copy-done.1), kind=kOutput, calls=%fused_computation.11 | convolution fusion | flops 14501806080 | bytes 38043648 | tf_op jit(solution)/shard_map/dot_general | solution.py:56
  (107 shorter events, 18.3 us)
Async XLA Ops:
  2.1 231.9 %all-to-all-start.1 = ((f32[1,128,32]{2,0,1:T(1,128)}), f32[1,128,32]{2,0,1:T(1,128)S(1)}, u32[]{:S(2)}, u32[]{:S(2)}) async-start(f32[1,128,32]{2,0,1:T(1,128)} %compare_convert_fusion), calls=%async_computation.1 | async-start | bytes 131072 | tf_op jit(solution)/shard_map/all_to_all | solution.py:138
  14.0 24.1 %copy-start.12 = (pred[32,1024]{1,0:T(8,128)(4,1)}, pred[32,1024]{1,0:T(8,128)(4,1)S(1)}, u32[]{:S(2)}) copy-start(pred[32,1024]{1,0:T(8,128)(4,1)S(1)} %iota_compare_fusion.17) | copy-start | bytes 98308
  14.9 46.6 %copy-start.11 = (f32[1,6,32,128]{3,1,2,0:T(8,128)}, f32[1,6,32,128]{3,1,2,0:T(8,128)S(1)}, u32[]{:S(2)}) copy-start(f32[1,6,32,128]{3,1,2,0:T(8,128)S(1)} %fusion.44) | copy-start | bytes 294916
  15.9 181.3 %collective-permute-start = (bf16[6,256]{1,0:T(8,128)(2,1)}, bf16[6,256]{1,0:T(8,128)(2,1)}, u32[]{:S(2)}, u32[]{:S(2)}) collective-permute-start(bf16[6,256]{1,0:T(8,128)(2,1)} %get-tuple-element.36), channel_id=1, source_target_pairs={{0,126},{1,127},{2,0},{3,1},{4,2},{5,3},{6,4},{7,5},{8,6},{9,7},{1... | collective-permute-start | bytes 9224 | tf_op jit(solution)/shard_map/ppermute | solution.py:12
  23.2 174.7 %collective-permute-start.1 = (bf16[6,256]{1,0:T(8,128)(2,1)}, bf16[6,256]{1,0:T(8,128)(2,1)S(1)}, u32[]{:S(2)}, u32[]{:S(2)}) collective-permute-start(bf16[6,256]{1,0:T(8,128)(2,1)} %get-tuple-element.35), channel_id=1, source_target_pairs={{0,127},{1,0},{2,1},{3,2},{4,3},{5,4},{6,5},{7,6},{8,7},{9,8},{10,... | collective-permute-start | bytes 9224 | tf_op jit(solution)/shard_map/ppermute | solution.py:12
  23.2 174.7 %collective-permute-start.2 = (bf16[6,256]{1,0:T(8,128)(2,1)}, bf16[6,256]{1,0:T(8,128)(2,1)S(1)}, u32[]{:S(2)}, u32[]{:S(2)}) collective-permute-start(bf16[6,256]{1,0:T(8,128)(2,1)} %get-tuple-element.34), channel_id=1, source_target_pairs={{0,1},{1,2},{2,3},{3,4},{4,5},{5,6},{6,7},{7,8},{8,9},{9,10},{10,1... | collective-permute-start | bytes 9224 | tf_op jit(solution)/shard_map/ppermute | solution.py:12
  23.7 174.3 %collective-permute-start.3 = (bf16[6,256]{1,0:T(8,128)(2,1)}, bf16[6,256]{1,0:T(8,128)(2,1)S(1)}, u32[]{:S(2)}, u32[]{:S(2)}) collective-permute-start(bf16[6,256]{1,0:T(8,128)(2,1)} %get-tuple-element.33), channel_id=1, source_target_pairs={{0,2},{1,3},{2,4},{3,5},{4,6},{5,7},{6,8},{7,9},{8,10},{9,11},{10,... | collective-permute-start | bytes 9224 | tf_op jit(solution)/shard_map/ppermute | solution.py:12
  27.3 15.6 %copy-start.17 = (s32[128,12]{0,1:T(8,128)S(1)}, s32[128,12]{0,1:T(8,128)}, u32[]{:S(2)}) copy-start(s32[128,12]{0,1:T(8,128)} %param.21) | copy-start | bytes 18436
  111.6 9.2 %copy-start.15 = (s32[32,512]{1,0:T(8,128)S(1)}, s32[32,512]{1,0:T(8,128)}, u32[]{:S(2)}) copy-start(s32[32,512]{1,0:T(8,128)} %param.18) | copy-start | bytes 196612
  121.2 20.4 %copy-start.9 = (f32[3,4096]{1,0:T(4,128)S(1)}, f32[3,4096]{1,0:T(4,128)}, u32[]{:S(2)}) copy-start(f32[3,4096]{1,0:T(4,128)} %param.15) | copy-start | bytes 147460
  121.2 20.4 %copy-start.10 = (f32[3,4096]{1,0:T(4,128)S(1)}, f32[3,4096]{1,0:T(4,128)}, u32[]{:S(2)}) copy-start(f32[3,4096]{1,0:T(4,128)} %param.14) | copy-start | bytes 147460
  181.2 16.0 %copy-start.16 = (bf16[6,5120]{1,0:T(8,128)(2,1)S(1)}, bf16[6,5120]{1,0:T(8,128)(2,1)}, u32[]{:S(2)}) copy-start(bf16[6,5120]{1,0:T(8,128)(2,1)} %fusion.48) | copy-start | bytes 184324
  233.4 0.7 copy-start.5
  234.1 39.1 %copy-start.13 = (pred[32,1024]{1,0:T(8,128)(4,1)S(1)}, pred[32,1024]{1,0:T(8,128)(4,1)}, u32[]{:S(2)}) copy-start(pred[32,1024]{1,0:T(8,128)(4,1)} %copy-done.12) | copy-start | bytes 98308
  234.1 41.9 %all-to-all-start = ((f32[72,128,32]{0,2,1:T(8,128)}), f32[72,128,32]{0,2,1:T(8,128)S(1)}, u32[]{:S(2)}, u32[]{:S(2)}) async-start(f32[72,128,32]{0,2,1:T(8,128)} %copy.66), calls=%async_computation | async-start | bytes 4194304 | tf_op jit(solution)/shard_map/all_to_all | solution.py:137
  242.9 30.2 %collective-permute-start.4 = (f32[6,256]{1,0:T(8,128)S(1)}, f32[6,256]{1,0:T(8,128)S(1)}, u32[]{:S(2)}, u32[]{:S(2)}) collective-permute-start(f32[6,256]{1,0:T(8,128)S(1)} %get-tuple-element.30), channel_id=1, source_target_pairs={{0,2},{1,3},{2,4},{3,5},{4,6},{5,7},{6,8},{7,9},{8,10},{9,11},{10,... | collective-permute-start | bytes 18440 | tf_op jit(solution)/shard_map/ppermute | solution.py:12
  244.1 29.1 %collective-permute-start.5 = (f32[6,256]{1,0:T(8,128)S(1)}, f32[6,256]{1,0:T(8,128)S(1)}, u32[]{:S(2)}, u32[]{:S(2)}) collective-permute-start(f32[6,256]{1,0:T(8,128)S(1)} %get-tuple-element.32), channel_id=1, source_target_pairs={{0,1},{1,2},{2,3},{3,4},{4,5},{5,6},{6,7},{7,8},{8,9},{9,10},{10,1... | collective-permute-start | bytes 18440 | tf_op jit(solution)/shard_map/ppermute | solution.py:12
  244.1 29.1 %collective-permute-start.6 = (f32[6,256]{1,0:T(8,128)S(1)}, f32[6,256]{1,0:T(8,128)S(1)}, u32[]{:S(2)}, u32[]{:S(2)}) collective-permute-start(f32[6,256]{1,0:T(8,128)S(1)} %get-tuple-element.31), channel_id=1, source_target_pairs={{0,127},{1,0},{2,1},{3,2},{4,3},{5,4},{6,5},{7,6},{8,7},{9,8},{10,... | collective-permute-start | bytes 18440 | tf_op jit(solution)/shard_map/ppermute | solution.py:12
  252.0 21.2 %collective-permute-start.7 = (f32[6,256]{1,0:T(8,128)S(1)}, f32[6,256]{1,0:T(8,128)S(1)}, u32[]{:S(2)}, u32[]{:S(2)}) collective-permute-start(f32[6,256]{1,0:T(8,128)S(1)} %bitcast.162), channel_id=1, source_target_pairs={{0,126},{1,127},{2,0},{3,1},{4,2},{5,3},{6,4},{7,5},{8,6},{9,7},{1... | collective-permute-start | bytes 18440 | tf_op jit(solution)/shard_map/ppermute | solution.py:12
  280.9 6.7 %copy-start.3 = (f32[4096,9]{0,1:T(8,128)S(1)}, f32[4096,9]{0,1:T(8,128)}, u32[]{:S(2)}) copy-start(f32[4096,9]{0,1:T(8,128)} %get-tuple-element.8) | copy-start | bytes 442372
  280.9 6.7 %copy-start.4 = (f32[4096,9]{0,1:T(8,128)S(1)}, f32[4096,9]{0,1:T(8,128)}, u32[]{:S(2)}) copy-start(f32[4096,9]{0,1:T(8,128)} %get-tuple-element.9) | copy-start | bytes 442372
  281.0 7.0 %slice-start = ((s8[5898240]{0:T(1024)(128)(4,1)}), s8[1703936]{0:T(1024)(128)(4,1)S(1)}, s32[]{:S(2)}) async-start(s8[5898240]{0:T(1024)(128)(4,1)} %bitcast.140), calls=%async_computation.3 | async-start | bytes 3407872
  283.3 4.3 %copy-start.8 = (f32[9,4096]{1,0:T(8,128)S(1)}, f32[9,4096]{1,0:T(8,128)}, u32[]{:S(2)}) copy-start(f32[9,4096]{1,0:T(8,128)} %param.27) | copy-start | bytes 442372
  283.4 4.6 %slice-start.1 = ((s8[5898240]{0:T(1024)(128)(4,1)}), s8[4194304]{0:T(1024)(128)(4,1)S(1)}, s32[]{:S(2)}) async-start(s8[5898240]{0:T(1024)(128)(4,1)} %bitcast.140), calls=%async_computation.4 | async-start | bytes 8388608
  300.0 56.3 %all-to-all-start.2 = ((f32[72,128,32]{0,2,1:T(8,128)}), f32[72,128,32]{0,2,1:T(8,128)S(1)}, u32[]{:S(2)}, u32[]{:S(2)}) async-start(f32[72,128,32]{0,2,1:T(8,128)} %bitcast.58), calls=%async_computation.2 | async-start | bytes 4194304 | tf_op jit(solution)/shard_map/all_to_all | solution.py:155
  304.9 5.3 %copy-start.2 = (s32[49152]{0:T(1024)S(1)}, s32[49152]{0:T(1024)}, u32[]{:S(2)}) copy-start(s32[49152]{0:T(1024)} %get-tuple-element.18) | copy-start | bytes 589828
  360.2 4.4 %copy-start = (pred[32,49152]{1,0:T(8,128)(4,1)S(1)}, pred[32,49152]{1,0:T(8,128)(4,1)}, u32[]{:S(2)}) copy-start(pred[32,49152]{1,0:T(8,128)(4,1)} %iota_compare_fusion.9) | copy-start | bytes 4718596
  364.5 4.3 %copy-start.1 = (s32[49152]{0:T(1024)S(1)}, s32[49152]{0:T(1024)}, u32[]{:S(2)}) copy-start(s32[49152]{0:T(1024)} %get-tuple-element.20) | copy-start | bytes 589828
  368.8 46.1 %copy-start.6 = (f32[6,5120]{1,0:T(8,128)S(1)}, f32[6,5120]{1,0:T(8,128)}, u32[]{:S(2)}) copy-start(f32[6,5120]{1,0:T(8,128)} %copy-done.5) | copy-start | bytes 368644
  368.8 46.1 %copy-start.7 = (f32[6,4096]{1,0:T(8,128)S(1)}, f32[6,4096]{1,0:T(8,128)}, u32[]{:S(2)}) copy-start(f32[6,4096]{1,0:T(8,128)} %reshape.638) | copy-start | bytes 294916
  368.8 46.1 %copy-start.14 = (f32[3,4096]{1,0:T(4,128)S(1)}, f32[3,4096]{1,0:T(4,128)}, u32[]{:S(2)}) copy-start(f32[3,4096]{1,0:T(4,128)} %param.16) | copy-start | bytes 147460
where the time goes:
time: 420 us; the launch traced here: 416 us
  matrix products  161 us (38%)
  local copies, waits for them, and re-layouts  145 us (35%)
  other arithmetic  49.8 us (12%)
  starting transfers between devices  43.3 us (10%)
  waiting for transfers between devices  15.1 us (4%)
    dot_general x4, matrix products, spread_columns(): jnp.dot(widened, lane_hits, preferred_element_type=jnp.float32, precision...  106 us
    dot_general x4, matrix products, select_columns(): jnp.dot(padded, lane_hits, preferred_element_type=jnp.float32, precision=...  45.2 us
    reshape x2, local copies, waits for them, and re-layouts, select_columns(): return result.reshape((row_count,) + positions.shape)  38.2 us
    unnamed x51, local copies, waits for them, and re-layouts  23 us
    ppermute x8, starting transfers between devices, shifted(): return lax.ppermute(value, axis, pairs)  18.5 us
    select_n x4, other arithmetic, spread_columns(): jnp.where(group_hits[None], flat_values[:, None, :], 0.0)  16.8 us
    ppermute x8, waiting for transfers between devices, shifted(): return lax.ppermute(value, axis, pairs)  15 us
    slice x3, local copies, waits for them, and re-layouts, device_work(): nearby[36:]  14.5 us
  transfers between devices with their start and end apart: 11, of which 1 were waited for; matrix products, arithmetic and copies ran while one was open for 65% of the time, Pallas kernels for 0%

commit v1 on v0

v1 whole, which is shorter than its diff:
```python
import jax
import jax.numpy as jnp
from jax import lax
from jax.experimental import pallas as pl
from jax.experimental.pallas import tpu as pltpu
from jax.sharding import PartitionSpec as P

REACH = 2
F32, BF16, I32 = jnp.float32, jnp.bfloat16, jnp.int32
LANES = 128
WIDE = 256
WORDS = 10
QUADS = 9
FACE = 12
LIMIT = 32767.0
VMEM_BYTES = 56 * 1024 * 1024


def offsets():
    return [move for move in range(-REACH, REACH + 1) if move != 0]


def shifted(value, axis, steps):
    count = lax.axis_size(axis)
    pairs = [(source, (source + steps) % count) for source in range(count)]
    return lax.ppermute(value, axis, pairs)


def indicator(row, count):
    number = lax.broadcasted_iota(I32, (count, row.shape[1]), 0)
    return jnp.where(number == row, 1.0, 0.0).astype(BF16)


def cut(value):
    high = value.astype(BF16)
    return high, (value - high.astype(F32)).astype(BF16)


def choose(wide, group, groups):
    total = jnp.where(group == 0, wide[0:8], 0.0)
    for g in range(1, groups):
        total = total + jnp.where(group == g, wide[8 * g : 8 * g + 8], 0.0)
    return total


def gather(parts, row, groups):
    hits = indicator(row & (WIDE - 1), WIDE)
    wide = jnp.dot(parts[0], hits, preferred_element_type=F32)
    for part in parts[1:]:
        wide = wide + jnp.dot(part, hits, preferred_element_type=F32)
    return choose(wide, row >> 8, groups)


def scatter(value, row, groups):
    high = value.astype(BF16).astype(F32)
    low = value - high
    group = row >> 8
    wide = []
    for g in range(groups):
        here = group == g
        wide += [jnp.where(here, high, 0.0), jnp.where(here, low, 0.0)]
    wide = jnp.concatenate(wide, 0).astype(BF16)
    hits = indicator(row & (WIDE - 1), WIDE)
    return across(wide, hits)


def across(left, right):
    return lax.dot_general(left, right, (((1,), (1,)), ((), ())), preferred_element_type=F32)


def fill_table(table, disp, direction):
    table[...] = jnp.zeros(table.shape, F32)
    for g in range(disp.shape[1] // WIDE):
        table[8 * g : 8 * g + 3, :] = disp[:, WIDE * g : WIDE * g + WIDE]
        table[8 * g + 3 : 8 * g + 6, :] = direction[:, WIDE * g : WIDE * g + WIDE]


def turn(v):
    lane = lax.broadcasted_iota(I32, v[0].shape, 1)
    low = lane < 64
    even = (lane & 32) == 0
    a0 = jnp.where(low, v[0], pltpu.roll(v[2], 64, 1))
    a2 = jnp.where(low, pltpu.roll(v[0], 64, 1), v[2])
    a1 = jnp.where(low, v[1], pltpu.roll(v[3], 64, 1))
    a3 = jnp.where(low, pltpu.roll(v[1], 64, 1), v[3])
    return [
        jnp.where(even, a0, pltpu.roll(a1, 32, 1)),
        jnp.where(even, pltpu.roll(a0, 96, 1), a1),
        jnp.where(even, a2, pltpu.roll(a3, 32, 1)),
        jnp.where(even, pltpu.roll(a2, 96, 1), a3),
    ]


def put_words(out, base, tails, words):
    for b, block in enumerate(turn([words[8 * q : 8 * q + 8] for q in range(4)])):
        out[pl.ds(base + WORDS * b, 8), :] = block
    tails[...] = words[32:40]


def put_tails(out, tails, count):
    for h in range(2):
        rows = turn([tails[pl.ds(4 * h + q, count, stride=8), :] for q in range(4)])
        for b in range(4):
            out[pl.ds(WORDS * b + 8 + h, count, stride=4 * WORDS), :] = rows[b]


def get_tails(source, tails, count):
    for h in range(2):
        rows = turn(
            [source[pl.ds(WORDS * b + 8 + h, count, stride=4 * WORDS), :] for b in range(4)]
        )
        for q in range(4):
            tails[pl.ds(4 * h + q, count, stride=8), :] = rows[q]


def get_words(source, base, tail):
    blocks = turn([source[pl.ds(base + WORDS * b, 8), :] for b in range(4)])
    return jnp.concatenate(blocks + [tail], 0)


def step_of(level):
    return jnp.exp(level.astype(F32) * (0.25 * 0.6931471805599453))


def level_of(values):
    top = jnp.max(jnp.abs(values), axis=0, keepdims=True)
    return jnp.ceil(jnp.log(jnp.maximum(top, 1e-30)) * (4.0 / 0.6931471805599453))


def split_words(words):
    second = (words << 16) >> 16
    first = (words - second) >> 16
    return first, second


def decode(words):
    out = []
    row = lax.broadcasted_iota(I32, (8, LANES), 0)
    halves = split_words(words)
    for half in halves:
        scale = step_of(half[36:37]) * (1.0 / LIMIT)
        value = half.astype(F32) * scale
        out.append(jnp.concatenate([value[:32], jnp.where(row < 4, value[32:40], 0.0)], 0))
    return out[0], out[1], halves[0][37:38].astype(F32)


def encode(values):
    level = level_of(values)
    code = jnp.round(values * (LIMIT / step_of(level)))
    row = lax.broadcasted_iota(I32, values.shape, 0)
    return jnp.where(row == 36, level, code)


def fold2(a, b, distance):
    row = lax.broadcasted_iota(I32, a.shape, 0)
    first = (row & distance) == 0
    return jnp.where(first, a, b) + pltpu.roll(jnp.where(first, b, a), 8 - distance, 0)


def fold(v):
    v = [fold2(v[2 * r], v[2 * r + 1], 1) for r in range(4)]
    v = [fold2(v[2 * r], v[2 * r + 1], 2) for r in range(2)]
    return fold2(v[0], v[1], 4)


def tail_rows(block):
    return jnp.concatenate([block, jnp.zeros((4, LANES), F32)], 0)


def contract(mortar, lane, first, second):
    sums = ([], [])
    for q in range(QUADS):
        pieces = [mortar[q, 8 * t : 8 * t + 8, lane : lane + LANES] for t in range(4)]
        pieces.append(tail_rows(mortar[q, 32:36, lane : lane + LANES]))
        for field, out in zip((first, second), sums):
            total = pieces[0] * field[0:8]
            for t in range(1, 5):
                total = total + pieces[t] * field[8 * t : 8 * t + 8]
            out.append(total)
    last = fold2(sums[0][8], sums[1][8], 1)
    last = last + pltpu.roll(last, 6, 0)
    last = last + pltpu.roll(last, 4, 0)
    return fold(sums[0][:8]), fold(sums[1][:8]), last


def adjoint(mortar, lane, weights):
    rows = [(weights[q : q + 1], weights[8 + q : 9 + q]) for q in range(8)]
    rows.append((weights[16:17], weights[17:18]))
    sums = []
    for t in range(5):
        pair = [None, None]
        for q in range(QUADS):
            if t < 4:
                piece = mortar[q, 8 * t : 8 * t + 8, lane : lane + LANES]
            else:
                piece = tail_rows(mortar[q, 32:36, lane : lane + LANES])
            for w in range(2):
                term = piece * rows[q][w]
                pair[w] = term if q == 0 else pair[w] + term
        sums.append(pair)
    return [jnp.concatenate([pair[w] for pair in sums], 0) for w in range(2)]


def fill_faces(faces, parts, nodes):
    for a in range(FACE):
        faces[pl.ds(a, 8, stride=FACE), :] = gather(parts, nodes[a : a + 1, :], 16)


def padded_fields(faces):
    pad = jnp.zeros((4, LANES), F32)
    return jnp.concatenate([faces[0:36], pad], 0), jnp.concatenate([faces[36:72], pad], 0)


def pack_kernel(disp, direction, halo, nodes, send, count, s0, s1, s2, s3, out, slots, table, faces, square, tails):
    fill_table(table, disp, direction)
    parts = cut(table[...])
    for o, piece in enumerate((s0, s1, s2, s3)):
        piece[...] = gather(parts[:1], halo[o : o + 1, :], 16)
    fill_faces(faces, parts, nodes)
    first, second = padded_fields(faces)
    row = lax.broadcasted_iota(I32, first.shape, 0)
    codes = [encode(first), encode(second)]
    codes[0] = jnp.where(row == 37, 1.0, codes[0])
    left = []
    for code in codes:
        high = jnp.floor(code * (1.0 / 256.0))
        left += [high, code - 256.0 * high]
    left = jnp.concatenate(left, 0).astype(BF16)
    square[...] = jnp.zeros(square.shape, I32)
    square[0:32, :] = send[...]
    square[32:33, :] = count[...]
    turned = square[...].T
    lane = lax.broadcasted_iota(I32, turned.shape, 1)
    square[...] = jnp.where(lane < turned[:, 32:33], turned, -1)
    lane = lax.broadcasted_iota(I32, (32, LANES), 1)
    rows = square[pl.ds(0, 32, stride=4), :]
    for b in range(1, 4):
        moved = pltpu.roll(square[pl.ds(b, 32, stride=4), :], 32 * b, 1)
        rows = jnp.where((lane >> 5) == b, moved, rows)
    slots[...] = rows

    def group_pair(i, carry):
        hits = [indicator(slots[pl.ds(2 * i + t, 1), :], LANES) for t in range(2)]
        wide = jnp.dot(left, jnp.concatenate(hits, 1), preferred_element_type=F32)
        for t in range(2):
            here = wide[:, LANES * t : LANES * t + LANES]
            first = (here[0:40] * 256.0 + here[40:80]).astype(I32)
            second = (here[80:120] * 256.0 + here[120:160]).astype(I32)
            base = pl.multiple_of(80 * i, 8) + 40 * t
            at = pl.multiple_of(16 * i, 8) + 8 * t
            put_words(out, base, tails.at[pl.ds(at, 8), :], (first << 16) + second)
        return carry

    lax.fori_loop(0, 16, group_pair, 0)
    put_tails(out, tails, 32)


def element_kernel(disp, direction, p0, p1, p2, p3, nodes, blocks, own, s0, s1, s2, s3, table, hits, x, y, held, sums, sems):
    chunk = blocks.shape[0] // sems.shape[0]
    copies = [
        pltpu.make_async_copy(
            blocks.at[pl.ds(chunk * n, chunk)], held.at[pl.ds(chunk * n, chunk)], sems.at[n]
        )
        for n in range(sems.shape[0])
    ]
    for copy in copies:
        copy.start()
    fill_table(table, disp, direction)
    for o, piece in enumerate((p0, p1, p2, p3)):
        table[8 * (16 + o) : 8 * (17 + o), :] = piece[...]
    coarse = table[...].astype(BF16)
    elements = nodes.shape[1]

    def gather_node(a, carry):
        for h in range(elements // WIDE):
            row = nodes[pl.ds(a, 1), WIDE * h : WIDE * h + WIDE]
            hit = indicator(row & (WIDE - 1), WIDE)
            at = pl.multiple_of(a * elements, WIDE) + WIDE * h
            hits[:, pl.ds(at, WIDE)] = hit
            wide = jnp.dot(coarse, hit, preferred_element_type=F32)
            picked = choose(wide, row >> 8, 20)
            for part in range(WIDE // LANES):
                x[2 * h + part, pl.ds(a, 8, stride=32), :] = picked[
                    :, LANES * part : LANES * part + LANES
                ]
        return carry

    lax.fori_loop(0, 32, gather_node, 0)
    y[...] = jnp.zeros(y.shape, F32)
    for n, copy in enumerate(copies):
        copy.wait()
        for part in range(elements // LANES):

            def eight_rows(i, carry, part=part, n=n):
                u, v = [], []
                for r in range(8):
                    block = held[
                        chunk * n + 8 * i + r, :, LANES * part : LANES * part + LANES
                    ].astype(F32)
                    for w, out in enumerate((u, v)):
                        total = block[0:8] * x[part, 96 * w : 96 * w + 8, :]
                        for t in range(1, 12):
                            total = total + block[8 * t : 8 * t + 8] * x[
                                part, 96 * w + 8 * t : 96 * w + 8 * t + 8, :
                            ]
                        out.append(total)
                at = pl.multiple_of(chunk * n + 8 * i, 8)
                y[part, pl.ds(at, 8), :] = fold(u)
                y[part, pl.ds(96 + at, 8), :] = fold(v)
                return carry

            lax.fori_loop(0, chunk // 8, eight_rows, 0)
    sums[...] = jnp.zeros(sums.shape, F32)

    def scatter_node(a, carry):
        for h in range(elements // WIDE):
            row = nodes[pl.ds(a, 1), WIDE * h : WIDE * h + WIDE] >> 8
            value = jnp.concatenate(
                [y[2 * h + part, pl.ds(a, 8, stride=32), :] for part in range(2)], 1
            )
            high = value.astype(BF16).astype(F32)
            low = value - high
            wide = []
            for g in range(20):
                here = row == g
                wide += [jnp.where(here, high, 0.0), jnp.where(here, low, 0.0)]
            wide = jnp.concatenate(wide, 0).astype(BF16)
            at = pl.multiple_of(a * elements, WIDE) + WIDE * h
            sums[...] += across(wide, hits[:, pl.ds(at, WIDE)])
        return carry

    lax.fori_loop(0, 32, scatter_node, 0)
    for g in range(16):
        own[8 * g : 8 * g + 8, :] = sums[16 * g : 16 * g + 8, :] + sums[16 * g + 8 : 16 * g + 16, :]
    for o, piece in enumerate((s0, s1, s2, s3)):
        g = 16 + o
        piece[...] = sums[16 * g : 16 * g + 8, :] + sums[16 * g + 8 : 16 * g + 16, :]


def near_kernel(disp, direction, nodes, pair, mortar, gap, out, table, faces, left):
    step = pl.program_id(0)

    @pl.when(step == 0)
    def _():
        fill_table(table, disp, direction)
        fill_faces(faces, cut(table[...]), nodes)
        first, second = padded_fields(faces)
        parts = cut(jnp.concatenate([first, second], 0))
        left[...] = jnp.concatenate(parts, 0)

    groups = out.shape[1] // LANES
    rows = [pair[pl.ds(step * groups + t, 1), :] for t in range(groups)]
    hits = jnp.concatenate([indicator(row, LANES) for row in rows], 1)
    wide = jnp.dot(left[...], hits, preferred_element_type=F32)
    wide = wide[:80] + wide[80:]
    number = lax.broadcasted_iota(I32, (8, LANES), 0)
    for t in range(groups):
        lane = LANES * t
        field = wide[:, lane : lane + LANES]
        opening, tangent, last = contract(mortar, lane, field[:40], field[40:])
        out[0:8, lane : lane + LANES] = opening + gap[0:8, lane : lane + LANES]
        out[8:16, lane : lane + LANES] = tangent
        extra = jnp.where((number & 1) == 0, gap[8:9, lane : lane + LANES], 0.0)
        out[16:24, lane : lane + LANES] = last + extra


def react(opening, tangent, live):
    fade = jnp.exp(-jnp.abs(opening))
    pressure = jnp.maximum(opening, 0.0) + jnp.log1p(fade)
    share = jnp.where(opening >= 0.0, 1.0, fade) / (1.0 + fade)
    return pressure * live, share * tangent * live


def far_kernel(arrived, near, mortar, out, weights, tails, back):
    groups = near.shape[1] // LANES
    get_tails(arrived, tails, groups)
    number = lax.broadcasted_iota(I32, (8, LANES), 0)
    for t in range(groups):
        lane = LANES * t
        words = get_words(arrived, 40 * t, tails[8 * t : 8 * t + 8, :])
        first, second, live = decode(words)
        opening, tangent, last = contract(mortar, lane, first, second)
        opening = opening + near[0:8, lane : lane + LANES]
        tangent = tangent + near[8:16, lane : lane + LANES]
        last = last + near[16:24, lane : lane + LANES]
        pressure, increment = react(opening, tangent, live)
        ninth = react(last[0:1], last[1:2], live)
        ninth = jnp.where((number & 1) == 0, ninth[0], ninth[1])
        here = jnp.concatenate([pressure, increment, ninth], 0)
        weights[:, lane : lane + LANES] = here
        first, second = (encode(force).astype(I32) for force in adjoint(mortar, lane, here))
        put_words(out, 40 * t, back.at[8 * t : 8 * t + 8, :], (first << 16) + second)
    put_tails(out, back, groups)


def add_faces(faces, nodes):
    total = None
    for a in range(FACE):
        term = scatter(faces[pl.ds(a, 8, stride=FACE), :], nodes[a : a + 1, :], 16)
        total = term if a == 0 else total + term
    return total


def merge(total, groups):
    return [total[16 * g : 16 * g + 8] + total[16 * g + 8 : 16 * g + 16] for g in range(groups)]


def slave_kernel(own, p0, p1, p2, p3, halo, nodes, pair, mortar, weights, out, sums, faces):
    step = pl.program_id(0)

    @pl.when(step == 0)
    def _():
        sums[...] = jnp.zeros(sums.shape, F32)

    groups = weights.shape[1] // LANES
    rows = [pair[pl.ds(step * groups + t, 1), :] for t in range(groups)]
    hits = jnp.concatenate([indicator(row, LANES) for row in rows], 1)
    forces = []
    for t in range(groups):
        lane = LANES * t
        force = jnp.concatenate(adjoint(mortar, lane, weights[:, lane : lane + LANES]), 0)
        forces.append(jnp.concatenate(cut(force), 0))
    sums[...] += across(jnp.concatenate(forces, 1), hits)

    @pl.when(step == pl.num_programs(0) - 1)
    def _():
        faces[...] = jnp.zeros(faces.shape, F32)
        faces[0:36, :] = sums[0:36, :] + sums[80:116, :]
        faces[36:72, :] = sums[40:76, :] + sums[120:156, :]
        total = add_faces(faces, nodes)
        for o, piece in enumerate((p0, p1, p2, p3)):
            total = total + scatter(piece[...], halo[o : o + 1, :], 16)
        for g, rows in enumerate(merge(total, 16)):
            out[8 * g : 8 * g + 8, :] = own[8 * g : 8 * g + 8, :] + rows


def last_kernel(arrived, slots, nodes, base, load, residual, applied, tails, forces, hits, faces):
    get_tails(arrived, tails, 32)

    def group(i, carry):
        at = pl.multiple_of(8 * i, 8)
        words = get_words(arrived, pl.multiple_of(40 * i, 8), tails[pl.ds(at, 8), :])
        first, second, _ = decode(words)
        force = jnp.concatenate([first, second], 0)
        lane = pl.multiple_of(LANES * i, LANES)
        forces[:, pl.ds(lane, LANES)] = jnp.concatenate(cut(force), 0)
        hits[:, pl.ds(lane, LANES)] = indicator(slots[pl.ds(i, 1), :], LANES)
        return carry

    lax.fori_loop(0, 32, group, 0)
    sums = across(forces[...], hits[...])
    faces[...] = jnp.zeros(faces.shape, F32)
    faces[0:36, :] = sums[0:36] + sums[80:116]
    faces[36:72, :] = sums[40:76] + sums[120:156]
    for g, rows in enumerate(merge(add_faces(faces, nodes), 16)):
        rows = rows + base[8 * g : 8 * g + 8, :]
        at = WIDE * g
        residual[:, at : at + WIDE] = load[:, at : at + WIDE] - rows[0:3]
        applied[:, at : at + WIDE] = rows[3:6]


def shape(dims, kind=F32):
    return jax.ShapeDtypeStruct(dims, kind)


def whole(dims):
    return pl.BlockSpec(dims, lambda *_: (0,) * len(dims))


def call(kernel, results, scratch, flops, size, **extra):
    return pl.pallas_call(
        kernel,
        out_shape=results,
        scratch_shapes=scratch,
        compiler_params=pltpu.CompilerParams(vmem_limit_bytes=VMEM_BYTES),
        cost_estimate=pl.CostEstimate(flops=flops, bytes_accessed=size, transcendentals=0),
        **extra,
    )


def on_device(
    disp,
    direction,
    load,
    blocks,
    elem_nodes,
    halo_send,
    master_nodes,
    slave_nodes,
    mortar_send,
    mortar_count,
    pair_slave,
    slave_mortar,
    master_mortar,
    gap_offset,
):
    peers = lax.axis_size("dom")
    moves = offsets()
    elements = elem_nodes.shape[1]
    pairs = pair_slave.shape[0]
    groups = pairs // LANES
    masters, slaves = master_nodes.T, slave_nodes.T
    send = mortar_send[0].T
    pair = pair_slave.reshape(groups, LANES)
    width = halo_send.shape[1]
    piece = shape((8, width))

    packed = call(
        pack_kernel,
        [piece] * 4 + [shape((WORDS * peers, LANES), I32), shape((groups, LANES), I32)],
        [
            pltpu.VMEM((128, WIDE), F32),
            pltpu.VMEM((96, LANES), F32),
            pltpu.VMEM((LANES, LANES), I32),
            pltpu.VMEM((8 * groups, LANES), I32),
        ],
        10**9,
        10**6,
    )(disp, direction, halo_send, masters, send, mortar_count)
    outgoing, words, slots = packed[:4], packed[4], packed[5]

    def exchange(value):
        value = value.reshape(peers, 1, WORDS * LANES)
        value = lax.all_to_all(value, "dom", split_axis=0, concat_axis=0, tiled=True)
        return value.reshape(WORDS * peers, LANES)

    pieces = [shifted(outgoing[o], "dom", moves[o]) for o in range(4)]
    arrived = exchange(words)

    block = 4 * LANES
    steps = pairs // block
    mortar_spec = pl.BlockSpec((QUADS, 36, block), lambda i: (0, 0, i))
    row_spec = pl.BlockSpec((24, block), lambda i: (0, i))
    word_spec = pl.BlockSpec((4 * 4 * WORDS, LANES), lambda i: (i, 0))

    near = call(
        near_kernel,
        shape((24, pairs)),
        [
            pltpu.VMEM((128, WIDE), F32),
            pltpu.VMEM((96, LANES), F32),
            pltpu.VMEM((160, LANES), BF16),
        ],
        10**9,
        6 * 10**6,
        grid=(steps,),
        in_specs=[
            whole(disp.shape),
            whole(direction.shape),
            whole(slaves.shape),
            whole(pair.shape),
            mortar_spec,
            pl.BlockSpec((QUADS, block), lambda i: (0, i)),
        ],
        out_specs=row_spec,
    )(disp, direction, slaves, pair, slave_mortar, gap_offset)

    vmem = pl.BlockSpec(memory_space=pltpu.VMEM)
    element = call(
        element_kernel,
        [shape((128, WIDE))] + [piece] * 4,
        [
            pltpu.VMEM((160, WIDE), F32),
            pltpu.VMEM((WIDE, 32 * elements), BF16),
            pltpu.VMEM((elements // LANES, 256, LANES), F32),
            pltpu.VMEM((elements // LANES, 256, LANES), F32),
            pltpu.VMEM(blocks.shape, BF16),
            pltpu.VMEM((320, WIDE), F32),
            pltpu.SemaphoreType.DMA((4,)),
        ],
        4 * 10**9,
        10**7,
        in_specs=[vmem] * 7 + [pl.BlockSpec(memory_space=pl.ANY)],
    )(disp, direction, *pieces, elem_nodes, blocks)
    own, sums = element[0], element[1:]
    shared = [shifted(sums[o], "dom", -moves[o]) for o in range(4)]

    back, weights = call(
        far_kernel,
        [shape(words.shape, I32), shape((24, pairs))],
        [pltpu.VMEM((32, LANES), I32), pltpu.VMEM((32, LANES), I32)],
        10**9,
        6 * 10**6,
        grid=(steps,),
        in_specs=[word_spec, row_spec, mortar_spec],
        out_specs=[word_spec, row_spec],
    )(arrived, near, master_mortar)
    returned = exchange(back)

    base = call(
        slave_kernel,
        shape((128, WIDE)),
        [pltpu.VMEM((160, LANES), F32), pltpu.VMEM((96, LANES), F32)],
        10**9,
        6 * 10**6,
        grid=(steps,),
        in_specs=[whole((128, WIDE))]
        + [whole((8, width))] * 4
        + [
            whole(halo_send.shape),
            whole(slaves.shape),
            whole(pair.shape),
            mortar_spec,
            row_spec,
        ],
        out_specs=whole((128, WIDE)),
    )(own, *shared, halo_send, slaves, pair, slave_mortar, weights)

    return call(
        last_kernel,
        [shape(load.shape), shape(load.shape)],
        [
            pltpu.VMEM((8 * groups, LANES), I32),
            pltpu.VMEM((160, pairs), BF16),
            pltpu.VMEM((LANES, pairs), BF16),
            pltpu.VMEM((96, LANES), F32),
        ],
        10**9,
        10**6,
    )(returned, slots, masters, base, load)


def solution(mesh):
    return jax.shard_map(
        on_device,
        mesh=mesh,
        in_specs=(
            P(None, "dom"),
            P(None, "dom"),
            P(None, "dom"),
            P(None, None, "dom"),
            P(None, "dom"),
            P("dom", None),
            P("dom", None),
            P("dom", None),
            P("dom", None, None),
            P("dom", None),
            P("dom"),
            P(None, None, "dom"),
            P(None, None, "dom"),
            P(None, "dom"),
        ),
        out_specs=(P(None, "dom"), P(None, "dom")),
        check_vma=False,
    )
```

time: 420 us -> 119 us (0.28)
  matrix products: 161 us -> 0 us
  local copies, waits for them, and re-layouts: 145 us -> 2.91 us
  Pallas kernels: 0 us -> 63.2 us
  other arithmetic: 49.8 us -> 0 us
  starting transfers between devices: 43.3 us -> 34 us
    dot_general x9 -> x0, matrix products: 161 us -> none  [the longest x4 106 us: spread_columns(): jnp.dot(widened, lane_hits, preferred_element_type=jnp.float32, precision...]
    pallas_call x0 -> x6, Pallas kernels: none -> 63.2 us  [the longest x1 22.7 us: on_device(): call(element_kernel, [shape((128, WIDE))] + [piece] * 4, [pltpu.VMEM((160...]
    reshape x12 -> x0, local copies, waits for them, and re-layouts: 47.3 us -> none  [the longest x2 38.2 us: select_columns(): return result.reshape((row_count,) + positions.shape)]
    gather x3 -> x0, local copies, waits for them, and re-layouts: 25.9 us -> none  [the longest x1 14.1 us: device_work(): slave_index = slave_nodes[pair_slave]]
    slice x8 -> x0, local copies, waits for them, and re-layouts: 22.5 us -> none  [the longest x3 14.5 us: device_work(): nearby[36:]]
    select_n x11 -> x0, other arithmetic: 20.4 us -> none  [the longest x4 16.8 us: spread_columns(): jnp.where(group_hits[None], flat_values[:, None, :], 0.0)]
    unnamed x51 -> x28, local copies, waits for them, and re-layouts: 23 us -> 2.91 us
    transpose x3 -> x0, local copies, waits for them, and re-layouts: 11.8 us -> none  [the longest x1 9.37 us: on_device(): select_columns(fields, master_index).transpose(0, 3, 1, 2)]
  transfers between devices with their start and end apart: 11 -> 10, of which waited for: 1 -> 5; matrix products, arithmetic and copies ran while one was open for 65% -> 0% of each run, Pallas kernels for 0% -> 32%
where the time goes in v1:
time: 119 us; the launch traced here: 118 us
  Pallas kernels  63.2 us (53%)
  starting transfers between devices  34 us (29%)
  waiting for transfers between devices  17.1 us (14%)
  local copies, waits for them, and re-layouts  2.91 us (2%)
    pallas_call x1, Pallas kernels, on_device(): call(element_kernel, [shape((128, WIDE))] + [piece] * 4, [pltpu.VMEM((160...  22.7 us
    ppermute x8, starting transfers between devices, shifted(): return lax.ppermute(value, axis, pairs)  18.2 us
    all_to_all x2, starting transfers between devices, exchange(): lax.all_to_all(value, 'dom', split_axis=0, concat_axis=0, tiled=True)  15.8 us
    ppermute x8, waiting for transfers between devices, shifted(): return lax.ppermute(value, axis, pairs)  9.89 us
    pallas_call x1, Pallas kernels, on_device(): call(far_kernel, [shape(words.shape, I32), shape((24, pairs))], [pltpu.VM...  8.96 us
    pallas_call x1, Pallas kernels, on_device(): call(last_kernel, [shape(load.shape), shape(load.shape)], [pltpu.VMEM((8...  8.62 us
    pallas_call x1, Pallas kernels, on_device(): call(near_kernel, shape((24, pairs)), [pltpu.VMEM((128, WIDE), F32), pltp...  7.82 us
    pallas_call x1, Pallas kernels, on_device(): call(slave_kernel, shape((128, WIDE)), [pltpu.VMEM((160, LANES), F32), pl...  7.58 us
  transfers between devices with their start and end apart: 10, of which 5 were waited for; matrix products, arithmetic and copies ran while one was open for 0% of the time, Pallas kernels for 32%

profile of v1, /device:TPU:0, one launch (start us, length us, event | category | flops | bytes accessed | tf_op | source)
XLA Modules:
  0.0 118.0 jit_solution(2621407884341606746)
XLA Ops:
  0.6 7.5 %shard_map.149 = (f32[8,256]{1,0:T(8,128)}, f32[8,256]{1,0:T(8,128)}, f32[8,256]{1,0:T(8,128)}, f32[8,256]{1,0:T(8,128)}, s32[1280,128]{1,0:T(8,128)}, /*index=5*/s32[32,128]{1,0:T(8,128)}) custom-call(f32[3,4096]{1,0:T(4,128)} %disp.5, f32[3,4096]{1,0:T(4,128)} %direction.5, s32[4,256]{1,0:T(4,128)} %halo.3, s32[12,128]{1,0:T(8,128)} %bitcast.19, ...), custom_call_target="tpu_custom_call" | custom-call | flops 1000000000 | bytes 1000000 | tf_op jit(solution)/shard_map/pallas_call | solution.py:508
  8.2 11.1 %all-to-all-start = ((s32[128,1,1280]{2,1,0:T(1,128)}), s32[128,1,1280]{2,1,0:T(1,128)S(1)}, u32[]{:S(2)}, u32[]{:S(2)}) async-start(s32[128,1,1280]{2,1,0:T(1,128)} %bitcast.13), calls=%async_computation | async-start | bytes 1310720 | tf_op jit(solution)/shard_map/all_to_all | solution.py:524
  19.3 0.0 copy-start.9
  19.3 0.0 copy-start.8
  19.4 0.0 copy-start.7
  19.4 0.0 copy-start.6
  19.4 7.8 %shard_map.150.near = f32[24,4096]{1,0:T(8,128)} custom-call(f32[3,4096]{1,0:T(4,128)} %disp.5, f32[3,4096]{1,0:T(4,128)} %direction.5, s32[12,128]{1,0:T(8,128)} %bitcast.16, s32[32,128]{1,0:T(8,128)} %bitcast.14, f32[9,36,4096]{2,1,0:T(8,128)} %mortar.5, f32[9,4096]{1,0:T(8,128)} %gap.1), custom_call_target="tpu_custom_call" | custom-call | flops 1000000000 | bytes 6000000 | tf_op jit(solution)/shard_map/pallas_call | solution.py:536
  27.2 7.2 %all-to-all-done = s32[128,1,1280]{2,1,0:T(1,128)S(1)} async-done(((s32[128,1,1280]{2,1,0:T(1,128)}), s32[128,1,1280]{2,1,0:T(1,128)S(1)}, u32[]{:S(2)}, u32[]{:S(2)}) %all-to-all-start) | async-done | bytes 655392 | tf_op jit(solution)/shard_map/all_to_all | solution.py:524
  34.4 0.0 copy-start
  34.4 0.9 copy-done
  35.3 9.0 %shard_map.151 = (s32[1280,128]{1,0:T(8,128)}, f32[24,4096]{1,0:T(8,128)}) custom-call(s32[1280,128]{1,0:T(8,128)} %bitcast.10, f32[24,4096]{1,0:T(8,128)} %shard_map.150.near, f32[9,36,4096]{2,1,0:T(8,128)} %mortar.4), custom_call_target="tpu_custom_call" | custom-call | flops 1000000000 | bytes 6000000 | tf_op jit(solution)/shard_map/pallas_call | solution.py:578
  44.3 4.6 %all-to-all-start.1 = ((s32[128,1,1280]{2,1,0:T(1,128)}), s32[128,1,1280]{2,1,0:T(1,128)S(1)}, u32[]{:S(2)}, u32[]{:S(2)}) async-start(s32[128,1,1280]{2,1,0:T(1,128)} %bitcast.12), calls=%async_computation.1 | async-start | bytes 1310720 | tf_op jit(solution)/shard_map/all_to_all | solution.py:524
  48.9 0.0 copy-done.9
  48.9 7.4 %collective-permute-start = (f32[8,256]{1,0:T(8,128)S(1)}, f32[8,256]{1,0:T(8,128)S(1)}, u32[]{:S(2)}, u32[]{:S(2)}) collective-permute-start(f32[8,256]{1,0:T(8,128)S(1)} %copy-done.9), channel_id=1, source_target_pairs={{0,126},{1,127},{2,0},{3,1},{4,2},{5,3},{6,4},{7,5},{8,6},{9,7},{1... | collective-permute-start | bytes 24584 | tf_op jit(solution)/shard_map/ppermute | solution.py:26
  56.3 0.0 copy-done.8
  56.3 0.1 collective-permute-start.1
  56.3 0.0 copy-done.7
  56.3 0.4 collective-permute-start.2
  56.8 0.0 copy-done.6
  56.8 1.1 collective-permute-start.3
  57.9 0.0 collective-permute-done.p0
  57.9 0.0 collective-permute-done.1.p1
  57.9 0.0 copy-start.11
  57.9 7.0 %collective-permute-done.2.p2 = f32[8,256]{1,0:T(8,128)S(1)} collective-permute-done((f32[8,256]{1,0:T(8,128)S(1)}, f32[8,256]{1,0:T(8,128)S(1)}, u32[]{:S(2)}, u32[]{:S(2)}) %collective-permute-start.2) | collective-permute-done | bytes 8224 | tf_op jit(solution)/shard_map/ppermute | solution.py:26
  64.9 1.0 collective-permute-done.3.p3
  65.9 0.0 copy-done.10
  65.9 0.0 copy-done.11
  65.9 0.0 copy-done.12
  65.9 0.0 copy-start.13
  65.9 0.6 copy-done.13
  66.5 22.7 %shard_map.152 = (f32[128,256]{1,0:T(8,128)}, f32[8,256]{1,0:T(8,128)}, f32[8,256]{1,0:T(8,128)}, f32[8,256]{1,0:T(8,128)}, f32[8,256]{1,0:T(8,128)}) custom-call(f32[3,4096]{1,0:T(4,128)} %disp.5, f32[3,4096]{1,0:T(4,128)} %direction.5, f32[8,256]{1,0:T(8,128)} %copy-done.10, f32[8,256]{1,0:T(8,128)} %copy-done.11, f32[8,256]{1,0:T(8,128)} %copy-done.12, ...), custom_call_target="tpu_custom_call" | custom-call | flops 4000000000 | bytes 10000000 | tf_op jit(solution)/shard_map/pallas_call | solution.py:559
  89.2 0.1 collective-permute-start.4
  89.2 0.2 collective-permute-start.5
  89.4 7.1 %collective-permute-start.6 = (f32[8,256]{1,0:T(8,128)}, f32[8,256]{1,0:T(8,128)S(1)}, u32[]{:S(2)}, u32[]{:S(2)}) collective-permute-start(f32[8,256]{1,0:T(8,128)} %get-tuple-element.25), channel_id=1, source_target_pairs={{0,127},{1,0},{2,1},{3,2},{4,3},{5,4},{6,5},{7,6},{8,7},{9,8},{10,... | collective-permute-start | bytes 24584 | tf_op jit(solution)/shard_map/ppermute | solution.py:26
  96.5 1.9 %collective-permute-start.7 = (f32[8,256]{1,0:T(8,128)}, f32[8,256]{1,0:T(8,128)S(1)}, u32[]{:S(2)}, u32[]{:S(2)}) collective-permute-start(f32[8,256]{1,0:T(8,128)} %get-tuple-element.26), channel_id=1, source_target_pairs={{0,126},{1,127},{2,0},{3,1},{4,2},{5,3},{6,4},{7,5},{8,6},{9,7},{1... | collective-permute-start | bytes 24584 | tf_op jit(solution)/shard_map/ppermute | solution.py:26
  98.4 0.1 collective-permute-done.4.p0
  98.5 0.0 collective-permute-done.5.p1
  98.5 0.0 collective-permute-done.6.p2
  98.5 0.0 copy-start.4
  98.6 1.8 %collective-permute-done.7.p3 = f32[8,256]{1,0:T(8,128)S(1)} collective-permute-done((f32[8,256]{1,0:T(8,128)}, f32[8,256]{1,0:T(8,128)S(1)}, u32[]{:S(2)}, u32[]{:S(2)}) %collective-permute-start.7) | collective-permute-done | bytes 8224 | tf_op jit(solution)/shard_map/ppermute | solution.py:26
  100.4 0.0 copy-done.2
  100.4 0.0 copy-done.3
  100.4 0.0 copy-done.4
  100.4 0.6 copy-done.5
  100.9 7.6 %shard_map.153.base = f32[128,256]{1,0:T(8,128)} custom-call(f32[128,256]{1,0:T(8,128)} %get-tuple-element.22.own, f32[8,256]{1,0:T(8,128)} %copy-done.2, f32[8,256]{1,0:T(8,128)} %copy-done.3, f32[8,256]{1,0:T(8,128)} %copy-done.4, f32[8,256]{1,0:T(8,128)} %copy-done.5, s32[4,256]{1,0:T(4,128)} %halo.3, s32[12,128]{1,0:T(8,128)} %bitcast.17, ...), custom_call_target="tpu_custom_call" | custom-call | flops 1000000000 | bytes 6000000 | tf_op jit(solution)/shard_map/pallas_call | solution.py:590
  108.5 0.0 all-to-all-done.1
  108.5 0.8 copy-done.1
  109.4 8.6 %shard_map.154 = (f32[3,4096]{1,0:T(4,128)}, f32[3,4096]{1,0:T(4,128)}) custom-call(s32[1280,128]{1,0:T(8,128)} %bitcast.11, s32[32,128]{1,0:T(8,128)} %get-tuple-element.17.slots, s32[12,128]{1,0:T(8,128)} %bitcast.20, f32[128,256]{1,0:T(8,128)} %shard_map.153.base, f32[3,4096]{1,0:T(4,128)} %load.1), custom_call_target="tpu_custom_call" | custom-call | flops 1000000000 | bytes 1000000 | tf_op jit(solution)/shard_map/pallas_call | solution.py:609
  (6 shorter events, 0.0 us)
Async XLA Ops:
  8.2 26.3 %all-to-all-start = ((s32[128,1,1280]{2,1,0:T(1,128)}), s32[128,1,1280]{2,1,0:T(1,128)S(1)}, u32[]{:S(2)}, u32[]{:S(2)}) async-start(s32[128,1,1280]{2,1,0:T(1,128)} %bitcast.13), calls=%async_computation | async-start | bytes 1310720 | tf_op jit(solution)/shard_map/all_to_all | solution.py:524
  19.3 29.6 %copy-start.9 = (f32[8,256]{1,0:T(8,128)S(1)}, f32[8,256]{1,0:T(8,128)}, u32[]{:S(2)}) copy-start(f32[8,256]{1,0:T(8,128)} %get-tuple-element.18) | copy-start | bytes 24580
  19.3 36.9 %copy-start.8 = (f32[8,256]{1,0:T(8,128)S(1)}, f32[8,256]{1,0:T(8,128)}, u32[]{:S(2)}) copy-start(f32[8,256]{1,0:T(8,128)} %get-tuple-element.19) | copy-start | bytes 24580
  19.4 37.0 %copy-start.7 = (f32[8,256]{1,0:T(8,128)S(1)}, f32[8,256]{1,0:T(8,128)}, u32[]{:S(2)}) copy-start(f32[8,256]{1,0:T(8,128)} %get-tuple-element.20) | copy-start | bytes 24580
  19.4 37.4 %copy-start.6 = (f32[8,256]{1,0:T(8,128)S(1)}, f32[8,256]{1,0:T(8,128)}, u32[]{:S(2)}) copy-start(f32[8,256]{1,0:T(8,128)} %get-tuple-element.21) | copy-start | bytes 24580
  34.4 0.9 copy-start
  44.3 64.3 %all-to-all-start.1 = ((s32[128,1,1280]{2,1,0:T(1,128)}), s32[128,1,1280]{2,1,0:T(1,128)S(1)}, u32[]{:S(2)}, u32[]{:S(2)}) async-start(s32[128,1,1280]{2,1,0:T(1,128)} %bitcast.12), calls=%async_computation.1 | async-start | bytes 1310720 | tf_op jit(solution)/shard_map/all_to_all | solution.py:524
  48.9 9.0 %collective-permute-start = (f32[8,256]{1,0:T(8,128)S(1)}, f32[8,256]{1,0:T(8,128)S(1)}, u32[]{:S(2)}, u32[]{:S(2)}) collective-permute-start(f32[8,256]{1,0:T(8,128)S(1)} %copy-done.9), channel_id=1, source_target_pairs={{0,126},{1,127},{2,0},{3,1},{4,2},{5,3},{6,4},{7,5},{8,6},{9,7},{1... | collective-permute-start | bytes 24584 | tf_op jit(solution)/shard_map/ppermute | solution.py:26
  56.3 1.6 %collective-permute-start.1 = (f32[8,256]{1,0:T(8,128)S(1)}, f32[8,256]{1,0:T(8,128)S(1)}, u32[]{:S(2)}, u32[]{:S(2)}) collective-permute-start(f32[8,256]{1,0:T(8,128)S(1)} %copy-done.8), channel_id=1, source_target_pairs={{0,127},{1,0},{2,1},{3,2},{4,3},{5,4},{6,5},{7,6},{8,7},{9,8},{10,... | collective-permute-start | bytes 24584 | tf_op jit(solution)/shard_map/ppermute | solution.py:26
  56.3 8.5 %collective-permute-start.2 = (f32[8,256]{1,0:T(8,128)S(1)}, f32[8,256]{1,0:T(8,128)S(1)}, u32[]{:S(2)}, u32[]{:S(2)}) collective-permute-start(f32[8,256]{1,0:T(8,128)S(1)} %copy-done.7), channel_id=1, source_target_pairs={{0,1},{1,2},{2,3},{3,4},{4,5},{5,6},{6,7},{7,8},{8,9},{9,10},{10,1... | collective-permute-start | bytes 24584 | tf_op jit(solution)/shard_map/ppermute | solution.py:26
  56.8 9.1 %collective-permute-start.3 = (f32[8,256]{1,0:T(8,128)S(1)}, f32[8,256]{1,0:T(8,128)S(1)}, u32[]{:S(2)}, u32[]{:S(2)}) collective-permute-start(f32[8,256]{1,0:T(8,128)S(1)} %copy-done.6), channel_id=1, source_target_pairs={{0,2},{1,3},{2,4},{3,5},{4,6},{5,7},{6,8},{7,9},{8,10},{9,11},{10,... | collective-permute-start | bytes 24584 | tf_op jit(solution)/shard_map/ppermute | solution.py:26
  57.9 8.0 %copy-start.10 = (f32[8,256]{1,0:T(8,128)}, f32[8,256]{1,0:T(8,128)S(1)}, u32[]{:S(2)}) copy-start(f32[8,256]{1,0:T(8,128)S(1)} %collective-permute-done.p0) | copy-start | bytes 24580
  57.9 8.0 %copy-start.11 = (f32[8,256]{1,0:T(8,128)}, f32[8,256]{1,0:T(8,128)S(1)}, u32[]{:S(2)}) copy-start(f32[8,256]{1,0:T(8,128)S(1)} %collective-permute-done.1.p1) | copy-start | bytes 24580
  64.9 1.0 copy-start.12
  65.9 0.6 copy-start.13
  89.2 9.4 %collective-permute-start.4 = (f32[8,256]{1,0:T(8,128)}, f32[8,256]{1,0:T(8,128)S(1)}, u32[]{:S(2)}, u32[]{:S(2)}) collective-permute-start(f32[8,256]{1,0:T(8,128)} %get-tuple-element.23), channel_id=1, source_target_pairs={{0,2},{1,3},{2,4},{3,5},{4,6},{5,7},{6,8},{7,9},{8,10},{9,11},{10,... | collective-permute-start | bytes 24584 | tf_op jit(solution)/shard_map/ppermute | solution.py:26
  89.2 9.3 %collective-permute-start.5 = (f32[8,256]{1,0:T(8,128)}, f32[8,256]{1,0:T(8,128)S(1)}, u32[]{:S(2)}, u32[]{:S(2)}) collective-permute-start(f32[8,256]{1,0:T(8,128)} %get-tuple-element.24), channel_id=1, source_target_pairs={{0,1},{1,2},{2,3},{3,4},{4,5},{5,6},{6,7},{7,8},{8,9},{9,10},{10,1... | collective-permute-start | bytes 24584 | tf_op jit(solution)/shard_map/ppermute | solution.py:26
  89.4 9.1 %collective-permute-start.6 = (f32[8,256]{1,0:T(8,128)}, f32[8,256]{1,0:T(8,128)S(1)}, u32[]{:S(2)}, u32[]{:S(2)}) collective-permute-start(f32[8,256]{1,0:T(8,128)} %get-tuple-element.25), channel_id=1, source_target_pairs={{0,127},{1,0},{2,1},{3,2},{4,3},{5,4},{6,5},{7,6},{8,7},{9,8},{10,... | collective-permute-start | bytes 24584 | tf_op jit(solution)/shard_map/ppermute | solution.py:26
  96.5 3.9 %collective-permute-start.7 = (f32[8,256]{1,0:T(8,128)}, f32[8,256]{1,0:T(8,128)S(1)}, u32[]{:S(2)}, u32[]{:S(2)}) collective-permute-start(f32[8,256]{1,0:T(8,128)} %get-tuple-element.26), channel_id=1, source_target_pairs={{0,126},{1,127},{2,0},{3,1},{4,2},{5,3},{6,4},{7,5},{8,6},{9,7},{1... | collective-permute-start | bytes 24584 | tf_op jit(solution)/shard_map/ppermute | solution.py:26
  98.5 1.8 %copy-start.2 = (f32[8,256]{1,0:T(8,128)}, f32[8,256]{1,0:T(8,128)S(1)}, u32[]{:S(2)}) copy-start(f32[8,256]{1,0:T(8,128)S(1)} %collective-permute-done.4.p0) | copy-start | bytes 24580
  98.5 1.8 %copy-start.3 = (f32[8,256]{1,0:T(8,128)}, f32[8,256]{1,0:T(8,128)S(1)}, u32[]{:S(2)}) copy-start(f32[8,256]{1,0:T(8,128)S(1)} %collective-permute-done.5.p1) | copy-start | bytes 24580
  98.5 1.8 %copy-start.4 = (f32[8,256]{1,0:T(8,128)}, f32[8,256]{1,0:T(8,128)S(1)}, u32[]{:S(2)}) copy-start(f32[8,256]{1,0:T(8,128)S(1)} %collective-permute-done.6.p2) | copy-start | bytes 24580
  100.4 0.6 copy-start.5
  108.5 0.8 copy-start.1

commit v2 on v1

--- a/solution.py
+++ b/solution.py
@@ -11,9 +11,11 @@
 WIDE = 256
 WORDS = 10
 QUADS = 9
+CHUNKS = 4
+UNROLL = 8
 FACE = 12
 LIMIT = 32767.0
-VMEM_BYTES = 56 * 1024 * 1024
+MIB = 1024 * 1024
 
 
 def offsets():
@@ -170,8 +172,8 @@
 def contract(mortar, lane, first, second):
     sums = ([], [])
     for q in range(QUADS):
-        pieces = [mortar[q, 8 * t : 8 * t + 8, lane : lane + LANES] for t in range(4)]
-        pieces.append(tail_rows(mortar[q, 32:36, lane : lane + LANES]))
+        pieces = [mortar[q, 8 * t : 8 * t + 8, pl.ds(lane, LANES)] for t in range(4)]
+        pieces.append(tail_rows(mortar[q, 32:36, pl.ds(lane, LANES)]))
         for field, out in zip((first, second), sums):
             total = pieces[0] * field[0:8]
             for t in range(1, 5):
@@ -191,9 +193,9 @@
         pair = [None, None]
         for q in range(QUADS):
             if t < 4:
-                piece = mortar[q, 8 * t : 8 * t + 8, lane : lane + LANES]
+                piece = mortar[q, 8 * t : 8 * t + 8, pl.ds(lane, LANES)]
             else:
-                piece = tail_rows(mortar[q, 32:36, lane : lane + LANES])
+                piece = tail_rows(mortar[q, 32:36, pl.ds(lane, LANES)])
             for w in range(2):
                 term = piece * rows[q][w]
                 pair[w] = term if q == 0 else pair[w] + term
@@ -251,7 +253,7 @@
             put_words(out, base, tails.at[pl.ds(at, 8), :], (first << 16) + second)
         return carry
 
-    lax.fori_loop(0, 16, group_pair, 0)
+    lax.fori_loop(0, 16, group_pair, 0, unroll=True)
     put_tails(out, tails, 32)
 
 
@@ -285,7 +287,7 @@
                 ]
         return carry
 
-    lax.fori_loop(0, 32, gather_node, 0)
+    lax.fori_loop(0, 32, gather_node, 0, unroll=8)
     y[...] = jnp.zeros(y.shape, F32)
     for n, copy in enumerate(copies):
         copy.wait()
@@ -329,7 +331,7 @@
             sums[...] += across(wide, hits[:, pl.ds(at, WIDE)])
         return carry
 
-    lax.fori_loop(0, 32, scatter_node, 0)
+    lax.fori_loop(0, 32, scatter_node, 0, unroll=8)
     for g in range(16):
         own[8 * g : 8 * g + 8, :] = sums[16 * g : 16 * g + 8, :] + sums[16 * g + 8 : 16 * g + 16, :]
     for o, piece in enumerate((s0, s1, s2, s3)):
@@ -337,32 +339,49 @@
         piece[...] = sums[16 * g : 16 * g + 8, :] + sums[16 * g + 8 : 16 * g + 16, :]
 
 
-def near_kernel(disp, direction, nodes, pair, mortar, gap, out, table, faces, left):
-    step = pl.program_id(0)
-
-    @pl.when(step == 0)
-    def _():
-        fill_table(table, disp, direction)
-        fill_faces(faces, cut(table[...]), nodes)
-        first, second = padded_fields(faces)
-        parts = cut(jnp.concatenate([first, second], 0))
-        left[...] = jnp.concatenate(parts, 0)
-
+def fetch(source, held, sems):
+    count = sems.shape[0]
+    part = source.shape[2] // count
+    copies = []
+    for n in range(count):
+        at = pl.ds(part * n, part)
+        copies.append(pltpu.make_async_copy(source.at[:, :, at], held.at[:, :, at], sems.at[n]))
+        copies[-1].start()
+    return copies
+
+
+def over_groups(copies, groups, body):
+    part = groups // len(copies)
+    for n, copy in enumerate(copies):
+        copy.wait()
+
+        def step(i, carry, n=n):
+            body(part * n + i, pl.multiple_of(LANES * (part * n + i), LANES))
+            return carry
+
+        lax.fori_loop(0, part, step, 0, unroll=UNROLL)
+
+
+def near_kernel(disp, direction, nodes, pair, gap, source, out, table, faces, fields, mortar, sems):
+    copies = fetch(source, mortar, sems)
+    fill_table(table, disp, direction)
+    fill_faces(faces, cut(table[...]), nodes)
+    left = jnp.concatenate(cut(jnp.concatenate(padded_fields(faces), 0)), 0)
     groups = out.shape[1] // LANES
-    rows = [pair[pl.ds(step * groups + t, 1), :] for t in range(groups)]
-    hits = jnp.concatenate([indicator(row, LANES) for row in rows], 1)
-    wide = jnp.dot(left[...], hits, preferred_element_type=F32)
-    wide = wide[:80] + wide[80:]
+    for i in range(groups // 2):
+        hits = [indicator(pair[2 * i + t : 2 * i + t + 1, :], LANES) for t in range(2)]
+        wide = jnp.dot(left, jnp.concatenate(hits, 1), preferred_element_type=F32)
+        fields[:, 2 * LANES * i : 2 * LANES * (i + 1)] = wide[:80] + wide[80:]
     number = lax.broadcasted_iota(I32, (8, LANES), 0)
-    for t in range(groups):
-        lane = LANES * t
-        field = wide[:, lane : lane + LANES]
-        opening, tangent, last = contract(mortar, lane, field[:40], field[40:])
-        out[0:8, lane : lane + LANES] = opening + gap[0:8, lane : lane + LANES]
-        out[8:16, lane : lane + LANES] = tangent
-        extra = jnp.where((number & 1) == 0, gap[8:9, lane : lane + LANES], 0.0)
-        out[16:24, lane : lane + LANES] = last + extra
-
+
+    def group(g, lane):
+        at = pl.ds(lane, LANES)
+        opening, tangent, last = contract(mortar, lane, fields.at[0:40, at], fields.at[40:80, at])
+        out[0:8, at] = opening + gap[0:8, at]
+        out[8:16, at] = tangent
+        out[16:24, at] = last + jnp.where((number & 1) == 0, gap[8:9, at], 0.0)
+
+    over_groups(copies, groups, group)
 
 def react(opening, tangent, live):
     fade = jnp.exp(-jnp.abs(opening))
@@ -371,27 +390,31 @@
     return pressure * live, share * tangent * live
 
 
-def far_kernel(arrived, near, mortar, out, weights, tails, back):
+def far_kernel(arrived, near, p0, p1, p2, p3, source, out, weights, tails, back, mortar, sems):
+    copies = fetch(source, mortar, sems)
     groups = near.shape[1] // LANES
     get_tails(arrived, tails, groups)
     number = lax.broadcasted_iota(I32, (8, LANES), 0)
-    for t in range(groups):
-        lane = LANES * t
-        words = get_words(arrived, 40 * t, tails[8 * t : 8 * t + 8, :])
-        first, second, live = decode(words)
+
+    def group(g, lane):
+        at = pl.ds(lane, LANES)
+        base = pl.multiple_of(40 * g, 8)
+        eight = pl.ds(pl.multiple_of(8 * g, 8), 8)
+        first, second, live = decode(get_words(arrived, base, tails[eight, :]))
         opening, tangent, last = contract(mortar, lane, first, second)
-        opening = opening + near[0:8, lane : lane + LANES]
-        tangent = tangent + near[8:16, lane : lane + LANES]
-        last = last + near[16:24, lane : lane + LANES]
+        opening = opening + near[0:8, at]
+        tangent = tangent + near[8:16, at]
+        last = last + near[16:24, at]
         pressure, increment = react(opening, tangent, live)
         ninth = react(last[0:1], last[1:2], live)
         ninth = jnp.where((number & 1) == 0, ninth[0], ninth[1])
         here = jnp.concatenate([pressure, increment, ninth], 0)
-        weights[:, lane : lane + LANES] = here
+        weights[:, at] = here
         first, second = (encode(force).astype(I32) for force in adjoint(mortar, lane, here))
-        put_words(out, 40 * t, back.at[8 * t : 8 * t + 8, :], (first << 16) + second)
+        put_words(out, base, back.at[eight, :], (first << 16) + second)
+
+    over_groups(copies, groups, group)
     put_tails(out, back, groups)
-
 
 def add_faces(faces, nodes):
     total = None
@@ -405,36 +428,29 @@
     return [total[16 * g : 16 * g + 8] + total[16 * g + 8 : 16 * g + 16] for g in range(groups)]
 
 
-def slave_kernel(own, p0, p1, p2, p3, halo, nodes, pair, mortar, weights, out, sums, faces):
-    step = pl.program_id(0)
-
-    @pl.when(step == 0)
-    def _():
-        sums[...] = jnp.zeros(sums.shape, F32)
-
+def slave_kernel(own, nodes, pair, weights, source, out, forces, hits, faces, mortar, sems):
+    copies = fetch(source, mortar, sems)
     groups = weights.shape[1] // LANES
-    rows = [pair[pl.ds(step * groups + t, 1), :] for t in range(groups)]
-    hits = jnp.concatenate([indicator(row, LANES) for row in rows], 1)
-    forces = []
-    for t in range(groups):
-        lane = LANES * t
-        force = jnp.concatenate(adjoint(mortar, lane, weights[:, lane : lane + LANES]), 0)
-        forces.append(jnp.concatenate(cut(force), 0))
-    sums[...] += across(jnp.concatenate(forces, 1), hits)
-
-    @pl.when(step == pl.num_programs(0) - 1)
-    def _():
-        faces[...] = jnp.zeros(faces.shape, F32)
-        faces[0:36, :] = sums[0:36, :] + sums[80:116, :]
-        faces[36:72, :] = sums[40:76, :] + sums[120:156, :]
-        total = add_faces(faces, nodes)
-        for o, piece in enumerate((p0, p1, p2, p3)):
-            total = total + scatter(piece[...], halo[o : o + 1, :], 16)
-        for g, rows in enumerate(merge(total, 16)):
-            out[8 * g : 8 * g + 8, :] = own[8 * g : 8 * g + 8, :] + rows
-
-
-def last_kernel(arrived, slots, nodes, base, load, residual, applied, tails, forces, hits, faces):
+
+    def group(g, lane):
+        at = pl.ds(lane, LANES)
+        force = jnp.concatenate(adjoint(mortar, lane, weights[:, at]), 0)
+        forces[:, at] = jnp.concatenate(cut(force), 0)
+        hits[:, at] = indicator(pair[pl.ds(g, 1), :], LANES)
+
+    over_groups(copies, groups, group)
+    sums = across(forces[...], hits[...])
+    for g, rows in enumerate(merge(face_sums(sums, faces, nodes), 16)):
+        out[8 * g : 8 * g + 8, :] = own[8 * g : 8 * g + 8, :] + rows
+
+
+def face_sums(sums, faces, nodes):
+    faces[...] = jnp.zeros(faces.shape, F32)
+    faces[0:36, :] = sums[0:36] + sums[80:116]
+    faces[36:72, :] = sums[40:76] + sums[120:156]
+    return add_faces(faces, nodes)
+
+def last_kernel(arrived, slots, nodes, base, p0, p1, p2, p3, halo, load, residual, applied, tails, forces, hits, faces):
     get_tails(arrived, tails, 32)
 
     def group(i, carry):
@@ -447,12 +463,11 @@
         hits[:, pl.ds(lane, LANES)] = indicator(slots[pl.ds(i, 1), :], LANES)
         return carry
 
-    lax.fori_loop(0, 32, group, 0)
-    sums = across(forces[...], hits[...])
-    faces[...] = jnp.zeros(faces.shape, F32)
-    faces[0:36, :] = sums[0:36] + sums[80:116]
-    faces[36:72, :] = sums[40:76] + sums[120:156]
-    for g, rows in enumerate(merge(add_faces(faces, nodes), 16)):
+    lax.fori_loop(0, 32, group, 0, unroll=16)
+    total = face_sums(across(forces[...], hits[...]), faces, nodes)
+    for o, piece in enumerate((p0, p1, p2, p3)):
+        total = total + scatter(piece[...], halo[o : o + 1, :], 16)
+    for g, rows in enumerate(merge(total, 16)):
         rows = rows + base[8 * g : 8 * g + 8, :]
         at = WIDE * g
         residual[:, at : at + WIDE] = load[:, at : at + WIDE] - rows[0:3]
@@ -463,19 +478,132 @@
     return jax.ShapeDtypeStruct(dims, kind)
 
 
-def whole(dims):
-    return pl.BlockSpec(dims, lambda *_: (0,) * len(dims))
-
-
-def call(kernel, results, scratch, flops, size, **extra):
+def settled(*arrays):
+    return [pltpu.with_memory_space_constraint(array, pltpu.HBM) for array in arrays]
+
+
+def call(kernel, results, scratch, flops, size, room, **extra):
     return pl.pallas_call(
         kernel,
         out_shape=results,
         scratch_shapes=scratch,
-        compiler_params=pltpu.CompilerParams(vmem_limit_bytes=VMEM_BYTES),
+        compiler_params=pltpu.CompilerParams(vmem_limit_bytes=room * MIB),
         cost_estimate=pl.CostEstimate(flops=flops, bytes_accessed=size, transcendentals=0),
         **extra,
     )
+
+
+def pack(disp, direction, halo_send, masters, send, count):
+    groups = send.shape[1] // 4
+    piece = shape((8, halo_send.shape[1]))
+    return call(
+        pack_kernel,
+        [piece] * 4 + [shape((WORDS * send.shape[1], LANES), I32), shape((groups, LANES), I32)],
+        [
+            pltpu.VMEM((128, WIDE), F32),
+            pltpu.VMEM((96, LANES), F32),
+            pltpu.VMEM((LANES, LANES), I32),
+            pltpu.VMEM((8 * groups, LANES), I32),
+        ],
+        10**9,
+        10**6,
+        8,
+    )(*settled(disp, direction, halo_send, masters, send, count))
+
+
+def inputs(count):
+    vmem = pl.BlockSpec(memory_space=pltpu.VMEM)
+    return [vmem] * count + [pl.BlockSpec(memory_space=pl.ANY)]
+
+
+def mortar_scratch(mortar):
+    return [pltpu.VMEM(mortar.shape, F32), pltpu.SemaphoreType.DMA((CHUNKS,))]
+
+
+def near_part(disp, direction, slaves, pair, mortar, gap):
+    pairs = mortar.shape[2]
+    return call(
+        near_kernel,
+        shape((24, pairs)),
+        [
+            pltpu.VMEM((128, WIDE), F32),
+            pltpu.VMEM((96, LANES), F32),
+            pltpu.VMEM((80, pairs), F32),
+        ]
+        + mortar_scratch(mortar),
+        10**9,
+        6 * 10**6,
+        14,
+        in_specs=inputs(5),
+    )(*settled(disp, direction, slaves, pair, gap, mortar))
+
+
+def elements_part(disp, direction, pieces, nodes, blocks):
+    elements = nodes.shape[1]
+    return call(
+        element_kernel,
+        [shape((128, WIDE))] + [shape((8, WIDE))] * 4,
+        [
+            pltpu.VMEM((160, WIDE), F32),
+            pltpu.VMEM((WIDE, 32 * elements), BF16),
+            pltpu.VMEM((elements // LANES, 256, LANES), F32),
+            pltpu.VMEM((elements // LANES, 256, LANES), F32),
+            pltpu.VMEM(blocks.shape, BF16),
+            pltpu.VMEM((320, WIDE), F32),
+            pltpu.SemaphoreType.DMA((4,)),
+        ],
+        4 * 10**9,
+        10**7,
+        32,
+        in_specs=inputs(7),
+    )(*settled(disp, direction), *pieces, *settled(nodes, blocks))
+
+
+def far_part(arrived, near, mortar, pieces):
+    pairs = mortar.shape[2]
+    tails = pltpu.VMEM((8 * (pairs // LANES), LANES), I32)
+    return call(
+        far_kernel,
+        [shape(arrived.shape, I32), shape((24, pairs))],
+        [tails, tails] + mortar_scratch(mortar),
+        10**9,
+        6 * 10**6,
+        14,
+        in_specs=inputs(6),
+    )(arrived, near, *pieces, *settled(mortar))
+
+
+def sum_scratch(pairs):
+    return [
+        pltpu.VMEM((160, pairs), BF16),
+        pltpu.VMEM((LANES, pairs), BF16),
+        pltpu.VMEM((96, LANES), F32),
+    ]
+
+
+def slave_part(own, slaves, pair, mortar, weights):
+    pairs = mortar.shape[2]
+    return call(
+        slave_kernel,
+        shape((128, WIDE)),
+        sum_scratch(pairs) + mortar_scratch(mortar),
+        10**9,
+        6 * 10**6,
+        14,
+        in_specs=inputs(4),
+    )(own, *settled(slaves, pair), weights, *settled(mortar))
+
+
+def last_part(returned, slots, masters, base, shared, halo_send, load):
+    groups = slots.shape[0]
+    return call(
+        last_kernel,
+        [shape(load.shape), shape(load.shape)],
+        [pltpu.VMEM((8 * groups, LANES), I32)] + sum_scratch(groups * LANES),
+        10**9,
+        10**6,
+        10,
+    )(returned, slots, *settled(masters), base, *shared, *settled(halo_send, load))
 
 
 def on_device(
@@ -496,128 +624,27 @@
 ):
     peers = lax.axis_size("dom")
     moves = offsets()
-    elements = elem_nodes.shape[1]
-    pairs = pair_slave.shape[0]
-    groups = pairs // LANES
     masters, slaves = master_nodes.T, slave_nodes.T
     send = mortar_send[0].T
-    pair = pair_slave.reshape(groups, LANES)
-    width = halo_send.shape[1]
-    piece = shape((8, width))
-
-    packed = call(
-        pack_kernel,
-        [piece] * 4 + [shape((WORDS * peers, LANES), I32), shape((groups, LANES), I32)],
-        [
-            pltpu.VMEM((128, WIDE), F32),
-            pltpu.VMEM((96, LANES), F32),
-            pltpu.VMEM((LANES, LANES), I32),
-            pltpu.VMEM((8 * groups, LANES), I32),
-        ],
-        10**9,
-        10**6,
-    )(disp, direction, halo_send, masters, send, mortar_count)
-    outgoing, words, slots = packed[:4], packed[4], packed[5]
+    pair = pair_slave.reshape(-1, LANES)
 
     def exchange(value):
         value = value.reshape(peers, 1, WORDS * LANES)
         value = lax.all_to_all(value, "dom", split_axis=0, concat_axis=0, tiled=True)
         return value.reshape(WORDS * peers, LANES)
 
+    packed = pack(disp, direction, halo_send, masters, send, mortar_count)
+    outgoing, words, slots = packed[:4], packed[4], packed[5]
+    arrived = exchange(words)
     pieces = [shifted(outgoing[o], "dom", moves[o]) for o in range(4)]
-    arrived = exchange(words)
-
-    block = 4 * LANES
-    steps = pairs // block
-    mortar_spec = pl.BlockSpec((QUADS, 36, block), lambda i: (0, 0, i))
-    row_spec = pl.BlockSpec((24, block), lambda i: (0, i))
-    word_spec = pl.BlockSpec((4 * 4 * WORDS, LANES), lambda i: (i, 0))
-
-    near = call(
-        near_kernel,
-        shape((24, pairs)),
-        [
-            pltpu.VMEM((128, WIDE), F32),
-            pltpu.VMEM((96, LANES), F32),
-            pltpu.VMEM((160, LANES), BF16),
-        ],
-        10**9,
-        6 * 10**6,
-        grid=(steps,),
-        in_specs=[
-            whole(disp.shape),
-            whole(direction.shape),
-            whole(slaves.shape),
-            whole(pair.shape),
-            mortar_spec,
-            pl.BlockSpec((QUADS, block), lambda i: (0, i)),
-        ],
-        out_specs=row_spec,
-    )(disp, direction, slaves, pair, slave_mortar, gap_offset)
-
-    vmem = pl.BlockSpec(memory_space=pltpu.VMEM)
-    element = call(
-        element_kernel,
-        [shape((128, WIDE))] + [piece] * 4,
-        [
-            pltpu.VMEM((160, WIDE), F32),
-            pltpu.VMEM((WIDE, 32 * elements), BF16),
-            pltpu.VMEM((elements // LANES, 256, LANES), F32),
-            pltpu.VMEM((elements // LANES, 256, LANES), F32),
-            pltpu.VMEM(blocks.shape, BF16),
-            pltpu.VMEM((320, WIDE), F32),
-            pltpu.SemaphoreType.DMA((4,)),
-        ],
-        4 * 10**9,
-        10**7,
-        in_specs=[vmem] * 7 + [pl.BlockSpec(memory_space=pl.ANY)],
-    )(disp, direction, *pieces, elem_nodes, blocks)
+    near = near_part(disp, direction, slaves, pair, slave_mortar, gap_offset)
+    element = elements_part(disp, direction, pieces, elem_nodes, blocks)
     own, sums = element[0], element[1:]
     shared = [shifted(sums[o], "dom", -moves[o]) for o in range(4)]
-
-    back, weights = call(
-        far_kernel,
-        [shape(words.shape, I32), shape((24, pairs))],
-        [pltpu.VMEM((32, LANES), I32), pltpu.VMEM((32, LANES), I32)],
-        10**9,
-        6 * 10**6,
-        grid=(steps,),
-        in_specs=[word_spec, row_spec, mortar_spec],
-        out_specs=[word_spec, row_spec],
-    )(arrived, near, master_mortar)
+    back, weights = far_part(arrived, near, master_mortar, pieces)
     returned = exchange(back)
-
-    base = call(
-        slave_kernel,
-        shape((128, WIDE)),
-        [pltpu.VMEM((160, LANES), F32), pltpu.VMEM((96, LANES), F32)],
-        10**9,
-        6 * 10**6,
-        grid=(steps,),
-        in_specs=[whole((128, WIDE))]
-        + [whole((8, width))] * 4
-        + [
-            whole(halo_send.shape),
-            whole(slaves.shape),
-            whole(pair.shape),
-            mortar_spec,
-            row_spec,
-        ],
-        out_specs=whole((128, WIDE)),
-    )(own, *shared, halo_send, slaves, pair, slave_mortar, weights)
-
-    return call(
-        last_kernel,
-        [shape(load.shape), shape(load.shape)],
-        [
-            pltpu.VMEM((8 * groups, LANES), I32),
-            pltpu.VMEM((160, pairs), BF16),
-            pltpu.VMEM((LANES, pairs), BF16),
-            pltpu.VMEM((96, LANES), F32),
-        ],
-        10**9,
-        10**6,
-    )(returned, slots, masters, base, load)
+    base = slave_part(own, slaves, pair, slave_mortar, weights)
+    return last_part(returned, slots, masters, base, shared, halo_send, load)
 
 
 def solution(mesh):

time: 119 us -> 76.7 us (0.64)
  Pallas kernels: 63.2 us -> 37.2 us
  waiting for transfers between devices: 17.1 us -> 3.94 us
  local copies, waits for them, and re-layouts: 2.91 us -> 0 us
    pallas_call x6, Pallas kernels: 63.2 us -> 37.2 us  [the longest x1 13.7 us: elements_part(): call(element_kernel, [shape((128, WIDE))] + [shape((8, WIDE))] * 4, [pltp...]
    all_to_all x2, waiting for transfers between devices: 7.24 us -> 0.01 us  [exchange(): lax.all_to_all(value, 'dom', split_axis=0, concat_axis=0, tiled=True)]
    ppermute x8, waiting for transfers between devices: 9.89 us -> 3.94 us  [shifted(): return lax.ppermute(value, axis, pairs)]
    unnamed x28 -> x0, local copies, waits for them, and re-layouts: 2.91 us -> none
  transfers between devices with their start and end apart: 10 -> 10, of which waited for: 5 -> 2; matrix products, arithmetic and copies ran while one was open for 0% -> 0% of each run, Pallas kernels for 32% -> 30%
where the time goes in v2:
time: 76.7 us; the launch traced here: 76.3 us
  Pallas kernels  37.2 us (49%)
  starting transfers between devices  34.4 us (45%)
  waiting for transfers between devices  3.94 us (5%)
    ppermute x8, starting transfers between devices, shifted(): return lax.ppermute(value, axis, pairs)  18.2 us
    all_to_all x2, starting transfers between devices, exchange(): lax.all_to_all(value, 'dom', split_axis=0, concat_axis=0, tiled=True)  16.3 us
    pallas_call x1, Pallas kernels, elements_part(): call(element_kernel, [shape((128, WIDE))] + [shape((8, WIDE))] * 4, [pltp...  13.7 us
    pallas_call x1, Pallas kernels, far_part(): call(far_kernel, [shape(arrived.shape, I32), shape((24, pairs))], [tails,...  6.11 us
    pallas_call x1, Pallas kernels, slave_part(): call(slave_kernel, shape((128, WIDE)), sum_scratch(pairs) + mortar_scratc...  5.4 us
    pallas_call x1, Pallas kernels, last_part(): call(last_kernel, [shape(load.shape), shape(load.shape)], [pltpu.VMEM((8...  4.59 us
    pallas_call x1, Pallas kernels, near_part(): call(near_kernel, shape((24, pairs)), [pltpu.VMEM((128, WIDE), F32), pltp...  4.11 us
    ppermute x8, waiting for transfers between devices, shifted(): return lax.ppermute(value, axis, pairs)  3.94 us
  transfers between devices with their start and end apart: 10, of which 2 were waited for; matrix products, arithmetic and copies ran while one was open for 0% of the time, Pallas kernels for 30%

profile of v2, /device:TPU:0, one launch (start us, length us, event | category | flops | bytes accessed | tf_op | source)
XLA Modules:
  0.0 76.3 jit_solution(10047946888444258514)
XLA Ops:
  0.6 3.3 %shard_map.149 = (f32[8,256]{1,0:T(8,128)S(1)}, f32[8,256]{1,0:T(8,128)S(1)}, f32[8,256]{1,0:T(8,128)S(1)}, f32[8,256]{1,0:T(8,128)S(1)}, s32[1280,128]{1,0:T(8,128)}, /*index=5*/s32[32,128]{1,0:T(8,128)S(1)}) custom-call(f32[3,4096]{1,0:T(4,128)} %disp.5, f32[3,4096]{1,0:T(4,128)} %direction.5, s32[4,256]{1,0:T(4,128)} %halo.3, s32[12,128]{1,0:T(8,128)} %bitcast.17, ...), custom_call_target="tpu_custom_call" | custom-call | flops 1000000000 | bytes 1000000 | tf_op jit(solution)/shard_map/pallas_call | solution.py:499
  4.0 11.1 %all-to-all-start = ((s32[128,1,1280]{2,1,0:T(1,128)}), s32[128,1,1280]{2,1,0:T(1,128)S(1)}, u32[]{:S(2)}, u32[]{:S(2)}) async-start(s32[128,1,1280]{2,1,0:T(1,128)} %bitcast.3), calls=%async_computation | async-start | bytes 1310720 | tf_op jit(solution)/shard_map/all_to_all | solution.py:633
  15.1 7.4 %collective-permute-start = (f32[8,256]{1,0:T(8,128)S(1)}, f32[8,256]{1,0:T(8,128)S(1)}, u32[]{:S(2)}, u32[]{:S(2)}) collective-permute-start(f32[8,256]{1,0:T(8,128)S(1)} %get-tuple-element.16), channel_id=1, source_target_pairs={{0,126},{1,127},{2,0},{3,1},{4,2},{5,3},{6,4},{7,5},{8,6},{9,7},{1... | collective-permute-start | bytes 24584 | tf_op jit(solution)/shard_map/ppermute | solution.py:28
  22.5 0.1 collective-permute-start.1
  22.6 0.4 collective-permute-start.2
  23.0 1.0 %collective-permute-start.3 = (f32[8,256]{1,0:T(8,128)S(1)}, f32[8,256]{1,0:T(8,128)S(1)}, u32[]{:S(2)}, u32[]{:S(2)}) collective-permute-start(f32[8,256]{1,0:T(8,128)S(1)} %get-tuple-element.19), channel_id=1, source_target_pairs={{0,2},{1,3},{2,4},{3,5},{4,6},{5,7},{6,8},{7,9},{8,10},{9,11},{10,... | collective-permute-start | bytes 24584 | tf_op jit(solution)/shard_map/ppermute | solution.py:28
  24.0 4.1 %shard_map.150.near = f32[24,4096]{1,0:T(8,128)S(1)} custom-call(f32[3,4096]{1,0:T(4,128)} %disp.5, f32[3,4096]{1,0:T(4,128)} %direction.5, s32[12,128]{1,0:T(8,128)} %bitcast.14, s32[32,128]{1,0:T(8,128)} %bitcast.12, f32[9,4096]{1,0:T(8,128)} %gap.1, f32[9,36,4096]{2,1,0:T(8,128)} %source.5), custom_call_target="tpu_custom_call" | custom-call | flops 1000000000 | bytes 6000000 | tf_op jit(solution)/shard_map/pallas_call | solution.py:525
  28.1 0.0 collective-permute-done.p0
  28.1 0.0 collective-permute-done.1.p1
  28.2 2.9 %collective-permute-done.2.p2 = f32[8,256]{1,0:T(8,128)S(1)} collective-permute-done((f32[8,256]{1,0:T(8,128)S(1)}, f32[8,256]{1,0:T(8,128)S(1)}, u32[]{:S(2)}, u32[]{:S(2)}) %collective-permute-start.2) | collective-permute-done | bytes 8224 | tf_op jit(solution)/shard_map/ppermute | solution.py:28
  31.1 1.0 %collective-permute-done.3.p3 = f32[8,256]{1,0:T(8,128)S(1)} collective-permute-done((f32[8,256]{1,0:T(8,128)S(1)}, f32[8,256]{1,0:T(8,128)S(1)}, u32[]{:S(2)}, u32[]{:S(2)}) %collective-permute-start.3) | collective-permute-done | bytes 8224 | tf_op jit(solution)/shard_map/ppermute | solution.py:28
  32.1 0.0 all-to-all-done
  32.1 6.1 %shard_map.151 = (s32[1280,128]{1,0:T(8,128)}, f32[24,4096]{1,0:T(8,128)S(1)}) custom-call(s32[1280,128]{1,0:T(8,128)S(1)} %bitcast.10, f32[24,4096]{1,0:T(8,128)S(1)} %shard_map.150.near, f32[8,256]{1,0:T(8,128)S(1)} %collective-permute-done.p0, f32[8,256]{1,0:T(8,128)S(1)} %collective-permute-done.1.p1, f32[8,256]{1,0:T(8,128)S(1)} %collective-permute-done.2.p2, ...), custom_call_target="tpu_custom_call" | custom-call | flops 1000000000 | bytes 6000000 | tf_op jit(solution)/shard_map/pallas_call | solution.py:565
  38.2 5.1 %all-to-all-start.1 = ((s32[128,1,1280]{2,1,0:T(1,128)}), s32[128,1,1280]{2,1,0:T(1,128)S(1)}, u32[]{:S(2)}, u32[]{:S(2)}) async-start(s32[128,1,1280]{2,1,0:T(1,128)} %bitcast.7), calls=%async_computation.1 | async-start | bytes 1310720 | tf_op jit(solution)/shard_map/all_to_all | solution.py:633
  43.3 13.7 %shard_map.152 = (f32[128,256]{1,0:T(8,128)S(1)}, f32[8,256]{1,0:T(8,128)S(1)}, f32[8,256]{1,0:T(8,128)S(1)}, f32[8,256]{1,0:T(8,128)S(1)}, f32[8,256]{1,0:T(8,128)S(1)}) custom-call(f32[3,4096]{1,0:T(4,128)} %disp.5, f32[3,4096]{1,0:T(4,128)} %direction.5, f32[8,256]{1,0:T(8,128)S(1)} %collective-permute-done.p0, f32[8,256]{1,0:T(8,128)S(1)} %collective-permute-done.1.p1, ...), custom_call_target="tpu_custom_call" | custom-call | flops 4000000000 | bytes 10000000 | tf_op jit(solution)/shard_map/pallas_call | solution.py:543
  57.0 1.0 %collective-permute-start.4 = (f32[8,256]{1,0:T(8,128)S(1)}, f32[8,256]{1,0:T(8,128)S(1)}, u32[]{:S(2)}, u32[]{:S(2)}) collective-permute-start(f32[8,256]{1,0:T(8,128)S(1)} %get-tuple-element.24), channel_id=1, source_target_pairs={{0,2},{1,3},{2,4},{3,5},{4,6},{5,7},{6,8},{7,9},{8,10},{9,11},{10,... | collective-permute-start | bytes 24584 | tf_op jit(solution)/shard_map/ppermute | solution.py:28
  58.0 0.0 collective-permute-start.5
  58.0 7.2 %collective-permute-start.6 = (f32[8,256]{1,0:T(8,128)S(1)}, f32[8,256]{1,0:T(8,128)S(1)}, u32[]{:S(2)}, u32[]{:S(2)}) collective-permute-start(f32[8,256]{1,0:T(8,128)S(1)} %get-tuple-element.26), channel_id=1, source_target_pairs={{0,127},{1,0},{2,1},{3,2},{4,3},{5,4},{6,5},{7,6},{8,7},{9,8},{10,... | collective-permute-start | bytes 24584 | tf_op jit(solution)/shard_map/ppermute | solution.py:28
  65.1 1.1 %collective-permute-start.7 = (f32[8,256]{1,0:T(8,128)S(1)}, f32[8,256]{1,0:T(8,128)S(1)}, u32[]{:S(2)}, u32[]{:S(2)}) collective-permute-start(f32[8,256]{1,0:T(8,128)S(1)} %get-tuple-element.27), channel_id=1, source_target_pairs={{0,126},{1,127},{2,0},{3,1},{4,2},{5,3},{6,4},{7,5},{8,6},{9,7},{1... | collective-permute-start | bytes 24584 | tf_op jit(solution)/shard_map/ppermute | solution.py:28
  66.3 5.4 %shard_map.153.base = f32[128,256]{1,0:T(8,128)S(1)} custom-call(f32[128,256]{1,0:T(8,128)S(1)} %get-tuple-element.22.own, s32[12,128]{1,0:T(8,128)} %bitcast.15, s32[32,128]{1,0:T(8,128)} %bitcast.13, f32[24,4096]{1,0:T(8,128)S(1)} %get-tuple-element.23.weights, f32[9,36,4096]{2,1,0:T(8,128)} %source.5), custom_call_target="tpu_custom_call" | custom-call | flops 1000000000 | bytes 6000000 | tf_op jit(solution)/shard_map/pallas_call | solution.py:586
  71.7 0.0 collective-permute-done.4.p0
  71.7 0.0 collective-permute-done.5.p1
  71.7 0.0 collective-permute-done.6.p2
  71.7 0.0 collective-permute-done.7.p3
  71.7 0.0 all-to-all-done.1
  71.7 4.6 %shard_map.154 = (f32[3,4096]{1,0:T(4,128)}, f32[3,4096]{1,0:T(4,128)}) custom-call(s32[1280,128]{1,0:T(8,128)S(1)} %bitcast.11, s32[32,128]{1,0:T(8,128)S(1)} %get-tuple-element.21.slots, s32[12,128]{1,0:T(8,128)} %bitcast.18, f32[128,256]{1,0:T(8,128)S(1)} %shard_map.153.base, f32[8,256]{1,0:T(8,128)S(1)} %collective-permute-done.4.p0, ...), custom_call_target="tpu_custom_call" | custom-call | flops 1000000000 | bytes 1000000 | tf_op jit(solution)/shard_map/pallas_call | solution.py:599
Async XLA Ops:
  4.0 28.1 %all-to-all-start = ((s32[128,1,1280]{2,1,0:T(1,128)}), s32[128,1,1280]{2,1,0:T(1,128)S(1)}, u32[]{:S(2)}, u32[]{:S(2)}) async-start(s32[128,1,1280]{2,1,0:T(1,128)} %bitcast.3), calls=%async_computation | async-start | bytes 1310720 | tf_op jit(solution)/shard_map/all_to_all | solution.py:633
  15.1 13.0 %collective-permute-start = (f32[8,256]{1,0:T(8,128)S(1)}, f32[8,256]{1,0:T(8,128)S(1)}, u32[]{:S(2)}, u32[]{:S(2)}) collective-permute-start(f32[8,256]{1,0:T(8,128)S(1)} %get-tuple-element.16), channel_id=1, source_target_pairs={{0,126},{1,127},{2,0},{3,1},{4,2},{5,3},{6,4},{7,5},{8,6},{9,7},{1... | collective-permute-start | bytes 24584 | tf_op jit(solution)/shard_map/ppermute | solution.py:28
  22.5 5.7 %collective-permute-start.1 = (f32[8,256]{1,0:T(8,128)S(1)}, f32[8,256]{1,0:T(8,128)S(1)}, u32[]{:S(2)}, u32[]{:S(2)}) collective-permute-start(f32[8,256]{1,0:T(8,128)S(1)} %get-tuple-element.17), channel_id=1, source_target_pairs={{0,127},{1,0},{2,1},{3,2},{4,3},{5,4},{6,5},{7,6},{8,7},{9,8},{10,... | collective-permute-start | bytes 24584 | tf_op jit(solution)/shard_map/ppermute | solution.py:28
  22.6 8.5 %collective-permute-start.2 = (f32[8,256]{1,0:T(8,128)S(1)}, f32[8,256]{1,0:T(8,128)S(1)}, u32[]{:S(2)}, u32[]{:S(2)}) collective-permute-start(f32[8,256]{1,0:T(8,128)S(1)} %get-tuple-element.18), channel_id=1, source_target_pairs={{0,1},{1,2},{2,3},{3,4},{4,5},{5,6},{6,7},{7,8},{8,9},{9,10},{10,1... | collective-permute-start | bytes 24584 | tf_op jit(solution)/shard_map/ppermute | solution.py:28
  23.0 9.1 %collective-permute-start.3 = (f32[8,256]{1,0:T(8,128)S(1)}, f32[8,256]{1,0:T(8,128)S(1)}, u32[]{:S(2)}, u32[]{:S(2)}) collective-permute-start(f32[8,256]{1,0:T(8,128)S(1)} %get-tuple-element.19), channel_id=1, source_target_pairs={{0,2},{1,3},{2,4},{3,5},{4,6},{5,7},{6,8},{7,9},{8,10},{9,11},{10,... | collective-permute-start | bytes 24584 | tf_op jit(solution)/shard_map/ppermute | solution.py:28
  38.2 33.5 %all-to-all-start.1 = ((s32[128,1,1280]{2,1,0:T(1,128)}), s32[128,1,1280]{2,1,0:T(1,128)S(1)}, u32[]{:S(2)}, u32[]{:S(2)}) async-start(s32[128,1,1280]{2,1,0:T(1,128)} %bitcast.7), calls=%async_computation.1 | async-start | bytes 1310720 | tf_op jit(solution)/shard_map/all_to_all | solution.py:633
  57.0 14.7 %collective-permute-start.4 = (f32[8,256]{1,0:T(8,128)S(1)}, f32[8,256]{1,0:T(8,128)S(1)}, u32[]{:S(2)}, u32[]{:S(2)}) collective-permute-start(f32[8,256]{1,0:T(8,128)S(1)} %get-tuple-element.24), channel_id=1, source_target_pairs={{0,2},{1,3},{2,4},{3,5},{4,6},{5,7},{6,8},{7,9},{8,10},{9,11},{10,... | collective-permute-start | bytes 24584 | tf_op jit(solution)/shard_map/ppermute | solution.py:28
  58.0 13.7 %collective-permute-start.5 = (f32[8,256]{1,0:T(8,128)S(1)}, f32[8,256]{1,0:T(8,128)S(1)}, u32[]{:S(2)}, u32[]{:S(2)}) collective-permute-start(f32[8,256]{1,0:T(8,128)S(1)} %get-tuple-element.25), channel_id=1, source_target_pairs={{0,1},{1,2},{2,3},{3,4},{4,5},{5,6},{6,7},{7,8},{8,9},{9,10},{10,1... | collective-permute-start | bytes 24584 | tf_op jit(solution)/shard_map/ppermute | solution.py:28
  58.0 13.7 %collective-permute-start.6 = (f32[8,256]{1,0:T(8,128)S(1)}, f32[8,256]{1,0:T(8,128)S(1)}, u32[]{:S(2)}, u32[]{:S(2)}) collective-permute-start(f32[8,256]{1,0:T(8,128)S(1)} %get-tuple-element.26), channel_id=1, source_target_pairs={{0,127},{1,0},{2,1},{3,2},{4,3},{5,4},{6,5},{7,6},{8,7},{9,8},{10,... | collective-permute-start | bytes 24584 | tf_op jit(solution)/shard_map/ppermute | solution.py:28
  65.1 6.6 %collective-permute-start.7 = (f32[8,256]{1,0:T(8,128)S(1)}, f32[8,256]{1,0:T(8,128)S(1)}, u32[]{:S(2)}, u32[]{:S(2)}) collective-permute-start(f32[8,256]{1,0:T(8,128)S(1)} %get-tuple-element.27), channel_id=1, source_target_pairs={{0,126},{1,127},{2,0},{3,1},{4,2},{5,3},{6,4},{7,5},{8,6},{9,7},{1... | collective-permute-start | bytes 24584 | tf_op jit(solution)/shard_map/ppermute | solution.py:28

commit v3 on v2

--- a/solution.py
+++ b/solution.py
@@ -11,8 +11,6 @@
 WIDE = 256
 WORDS = 10
 QUADS = 9
-CHUNKS = 4
-UNROLL = 8
 FACE = 12
 LIMIT = 32767.0
 MIB = 1024 * 1024
@@ -29,8 +27,8 @@
 
 
 def indicator(row, count):
-    number = lax.broadcasted_iota(I32, (count, row.shape[1]), 0)
-    return jnp.where(number == row, 1.0, 0.0).astype(BF16)
+    number = lax.broadcasted_iota(jnp.int16, (count, row.shape[1]), 0)
+    return jnp.where(number == row.astype(jnp.int16), jnp.ones((), BF16), jnp.zeros((), BF16))
 
 
 def cut(value):
@@ -53,15 +51,15 @@
     return choose(wide, row >> 8, groups)
 
 
+def place(value, group, groups):
+    both = jnp.concatenate(cut(value), 0)
+    group = jnp.broadcast_to(group, both.shape).astype(jnp.int16)
+    zero = jnp.zeros(both.shape, BF16)
+    return jnp.concatenate([jnp.where(group == g, both, zero) for g in range(groups)], 0)
+
+
 def scatter(value, row, groups):
-    high = value.astype(BF16).astype(F32)
-    low = value - high
-    group = row >> 8
-    wide = []
-    for g in range(groups):
-        here = group == g
-        wide += [jnp.where(here, high, 0.0), jnp.where(here, low, 0.0)]
-    wide = jnp.concatenate(wide, 0).astype(BF16)
+    wide = place(value, row >> 8, groups)
     hits = indicator(row & (WIDE - 1), WIDE)
     return across(wide, hits)
 
@@ -288,7 +286,7 @@
         return carry
 
     lax.fori_loop(0, 32, gather_node, 0, unroll=8)
-    y[...] = jnp.zeros(y.shape, F32)
+    y[:, 192:256, :] = jnp.zeros((y.shape[0], 64, LANES), F32)
     for n, copy in enumerate(copies):
         copy.wait()
         for part in range(elements // LANES):
@@ -311,7 +309,7 @@
                 y[part, pl.ds(96 + at, 8), :] = fold(v)
                 return carry
 
-            lax.fori_loop(0, chunk // 8, eight_rows, 0)
+            lax.fori_loop(0, chunk // 8, eight_rows, 0, unroll=3)
     sums[...] = jnp.zeros(sums.shape, F32)
 
     def scatter_node(a, carry):
@@ -320,13 +318,7 @@
             value = jnp.concatenate(
                 [y[2 * h + part, pl.ds(a, 8, stride=32), :] for part in range(2)], 1
             )
-            high = value.astype(BF16).astype(F32)
-            low = value - high
-            wide = []
-            for g in range(20):
-                here = row == g
-                wide += [jnp.where(here, high, 0.0), jnp.where(here, low, 0.0)]
-            wide = jnp.concatenate(wide, 0).astype(BF16)
+            wide = place(value, row, 20)
             at = pl.multiple_of(a * elements, WIDE) + WIDE * h
             sums[...] += across(wide, hits[:, pl.ds(at, WIDE)])
         return carry
@@ -359,7 +351,7 @@
             body(part * n + i, pl.multiple_of(LANES * (part * n + i), LANES))
             return carry
 
-        lax.fori_loop(0, part, step, 0, unroll=UNROLL)
+        lax.fori_loop(0, part, step, 0, unroll=True)
 
 
 def near_kernel(disp, direction, nodes, pair, gap, source, out, table, faces, fields, mortar, sems):
@@ -463,7 +455,7 @@
         hits[:, pl.ds(lane, LANES)] = indicator(slots[pl.ds(i, 1), :], LANES)
         return carry
 
-    lax.fori_loop(0, 32, group, 0, unroll=16)
+    lax.fori_loop(0, 32, group, 0, unroll=True)
     total = face_sums(across(forces[...], hits[...]), faces, nodes)
     for o, piece in enumerate((p0, p1, p2, p3)):
         total = total + scatter(piece[...], halo[o : o + 1, :], 16)
@@ -516,8 +508,8 @@
     return [vmem] * count + [pl.BlockSpec(memory_space=pl.ANY)]
 
 
-def mortar_scratch(mortar):
-    return [pltpu.VMEM(mortar.shape, F32), pltpu.SemaphoreType.DMA((CHUNKS,))]
+def mortar_scratch(mortar, stretches):
+    return [pltpu.VMEM(mortar.shape, F32), pltpu.SemaphoreType.DMA((stretches,))]
 
 
 def near_part(disp, direction, slaves, pair, mortar, gap):
@@ -530,7 +522,7 @@
             pltpu.VMEM((96, LANES), F32),
             pltpu.VMEM((80, pairs), F32),
         ]
-        + mortar_scratch(mortar),
+        + mortar_scratch(mortar, 8),
         10**9,
         6 * 10**6,
         14,
@@ -565,12 +557,12 @@
     return call(
         far_kernel,
         [shape(arrived.shape, I32), shape((24, pairs))],
-        [tails, tails] + mortar_scratch(mortar),
+        [tails, tails] + mortar_scratch(mortar, 4),
         10**9,
         6 * 10**6,
         14,
         in_specs=inputs(6),
-    )(arrived, near, *pieces, *settled(mortar))
+    )(arrived, near, pieces[2], pieces[3], pieces[0], pieces[1], *settled(mortar))
 
 
 def sum_scratch(pairs):
@@ -586,7 +578,7 @@
     return call(
         slave_kernel,
         shape((128, WIDE)),
-        sum_scratch(pairs) + mortar_scratch(mortar),
+        sum_scratch(pairs) + mortar_scratch(mortar, 8),
         10**9,
         6 * 10**6,
         14,
@@ -636,7 +628,8 @@
     packed = pack(disp, direction, halo_send, masters, send, mortar_count)
     outgoing, words, slots = packed[:4], packed[4], packed[5]
     arrived = exchange(words)
-    pieces = [shifted(outgoing[o], "dom", moves[o]) for o in range(4)]
+    received = {o: shifted(outgoing[o], "dom", moves[o]) for o in (2, 3, 0, 1)}
+    pieces = [received[o] for o in range(4)]
     near = near_part(disp, direction, slaves, pair, slave_mortar, gap_offset)
     element = elements_part(disp, direction, pieces, elem_nodes, blocks)
     own, sums = element[0], element[1:]

time: 76.7 us -> 72 us (0.939)
  Pallas kernels: 37.2 us -> 34.3 us
  waiting for transfers between devices: 3.94 us -> 2.44 us
    pallas_call x1, Pallas kernels: 13.7 us -> 11.6 us  [elements_part(): call(element_kernel, [shape((128, WIDE))] + [shape((8, WIDE))] * 4, [pltp...]
    ppermute x8, waiting for transfers between devices: 3.94 us -> 1.92 us  [shifted(): return lax.ppermute(value, axis, pairs)]
  transfers between devices with their start and end apart: 10 -> 10, of which waited for: 2 -> 3; matrix products, arithmetic and copies ran while one was open for 0% -> 0% of each run, Pallas kernels for 30% -> 29%
where the time goes in v3:
time: 72 us; the launch traced here: 71.5 us
  Pallas kernels  34.3 us (48%)
  starting transfers between devices  34.1 us (47%)
  waiting for transfers between devices  2.44 us (3%)
  between operations  0.73 us (1%)
    ppermute x8, starting transfers between devices, shifted(): return lax.ppermute(value, axis, pairs)  18.1 us
    all_to_all x2, starting transfers between devices, exchange(): lax.all_to_all(value, 'dom', split_axis=0, concat_axis=0, tiled=True)  16 us
    pallas_call x1, Pallas kernels, elements_part(): call(element_kernel, [shape((128, WIDE))] + [shape((8, WIDE))] * 4, [pltp...  11.6 us
    pallas_call x1, Pallas kernels, far_part(): call(far_kernel, [shape(arrived.shape, I32), shape((24, pairs))], [tails,...  6.11 us
    pallas_call x1, Pallas kernels, slave_part(): call(slave_kernel, shape((128, WIDE)), sum_scratch(pairs) + mortar_scratc...  5.26 us
    pallas_call x1, Pallas kernels, last_part(): call(last_kernel, [shape(load.shape), shape(load.shape)], [pltpu.VMEM((8...  4.21 us
    pallas_call x1, Pallas kernels, near_part(): call(near_kernel, shape((24, pairs)), [pltpu.VMEM((128, WIDE), F32), pltp...  4 us
    pallas_call x1, Pallas kernels, pack(): call(pack_kernel, [piece] * 4 + [shape((WORDS * send.shape[1], LANES), I3...  3.16 us
  transfers between devices with their start and end apart: 10, of which 3 were waited for; matrix products, arithmetic and copies ran while one was open for 0% of the time, Pallas kernels for 29%

profile of v3, /device:TPU:0, one launch (start us, length us, event | category | flops | bytes accessed | tf_op | source)
XLA Modules:
  0.0 71.5 jit_solution(13215016755425026806)
XLA Ops:
  0.6 3.2 %shard_map.149 = (f32[8,256]{1,0:T(8,128)S(1)}, f32[8,256]{1,0:T(8,128)S(1)}, f32[8,256]{1,0:T(8,128)S(1)}, f32[8,256]{1,0:T(8,128)S(1)}, s32[1280,128]{1,0:T(8,128)}, /*index=5*/s32[32,128]{1,0:T(8,128)S(1)}) custom-call(f32[3,4096]{1,0:T(4,128)} %disp.5, f32[3,4096]{1,0:T(4,128)} %direction.5, s32[4,256]{1,0:T(4,128)} %halo.3, s32[12,128]{1,0:T(8,128)} %bitcast.17, ...), custom_call_target="tpu_custom_call" | custom-call | flops 1000000000 | bytes 1000000 | tf_op jit(solution)/shard_map/pallas_call | solution.py:491
  3.8 11.1 %all-to-all-start = ((s32[128,1,1280]{2,1,0:T(1,128)}), s32[128,1,1280]{2,1,0:T(1,128)S(1)}, u32[]{:S(2)}, u32[]{:S(2)}) async-start(s32[128,1,1280]{2,1,0:T(1,128)} %bitcast.3), calls=%async_computation | async-start | bytes 1310720 | tf_op jit(solution)/shard_map/all_to_all | solution.py:625
  14.9 0.1 collective-permute-start
  15.0 1.2 %collective-permute-start.1 = (f32[8,256]{1,0:T(8,128)S(1)}, f32[8,256]{1,0:T(8,128)S(1)}, u32[]{:S(2)}, u32[]{:S(2)}) collective-permute-start(f32[8,256]{1,0:T(8,128)S(1)} %get-tuple-element.17), channel_id=1, source_target_pairs={{0,2},{1,3},{2,4},{3,5},{4,6},{5,7},{6,8},{7,9},{8,10},{9,11},{10,... | collective-permute-start | bytes 24584 | tf_op jit(solution)/shard_map/ppermute | solution.py:26
  16.2 6.3 %collective-permute-start.2 = (f32[8,256]{1,0:T(8,128)S(1)}, f32[8,256]{1,0:T(8,128)S(1)}, u32[]{:S(2)}, u32[]{:S(2)}) collective-permute-start(f32[8,256]{1,0:T(8,128)S(1)} %get-tuple-element.18), channel_id=1, source_target_pairs={{0,126},{1,127},{2,0},{3,1},{4,2},{5,3},{6,4},{7,5},{8,6},{9,7},{1... | collective-permute-start | bytes 24584 | tf_op jit(solution)/shard_map/ppermute | solution.py:26
  22.6 1.2 %collective-permute-start.3 = (f32[8,256]{1,0:T(8,128)S(1)}, f32[8,256]{1,0:T(8,128)S(1)}, u32[]{:S(2)}, u32[]{:S(2)}) collective-permute-start(f32[8,256]{1,0:T(8,128)S(1)} %get-tuple-element.19), channel_id=1, source_target_pairs={{0,127},{1,0},{2,1},{3,2},{4,3},{5,4},{6,5},{7,6},{8,7},{9,8},{10,... | collective-permute-start | bytes 24584 | tf_op jit(solution)/shard_map/ppermute | solution.py:26
  23.8 4.0 %shard_map.150.near = f32[24,4096]{1,0:T(8,128)S(1)} custom-call(f32[3,4096]{1,0:T(4,128)} %disp.5, f32[3,4096]{1,0:T(4,128)} %direction.5, s32[12,128]{1,0:T(8,128)} %bitcast.14, s32[32,128]{1,0:T(8,128)} %bitcast.12, f32[9,4096]{1,0:T(8,128)} %gap.1, f32[9,36,4096]{2,1,0:T(8,128)} %source.5), custom_call_target="tpu_custom_call" | custom-call | flops 1000000000 | bytes 6000000 | tf_op jit(solution)/shard_map/pallas_call | solution.py:517
  27.8 1.4 %collective-permute-done.p0.p2 = f32[8,256]{1,0:T(8,128)S(1)} collective-permute-done((f32[8,256]{1,0:T(8,128)S(1)}, f32[8,256]{1,0:T(8,128)S(1)}, u32[]{:S(2)}, u32[]{:S(2)}) %collective-permute-start) | collective-permute-done | bytes 8224 | tf_op jit(solution)/shard_map/ppermute | solution.py:26
  29.2 0.5 collective-permute-done.1.p1.p3
  29.7 0.0 collective-permute-done.2.p2.p0
  29.7 0.0 collective-permute-done.3.p3.p1
  29.7 0.5 all-to-all-done
  30.2 6.1 %shard_map.151 = (s32[1280,128]{1,0:T(8,128)}, f32[24,4096]{1,0:T(8,128)S(1)}) custom-call(s32[1280,128]{1,0:T(8,128)S(1)} %bitcast.10, f32[24,4096]{1,0:T(8,128)S(1)} %shard_map.150.near, f32[8,256]{1,0:T(8,128)S(1)} %collective-permute-done.p0.p2, f32[8,256]{1,0:T(8,128)S(1)} %collective-permute-done.1.p1.p3, f32[8,256]{1,0:T(8,128)S(1)} %collective-permute-done.2.p2.p0, ...), custom_call_target="tpu_custom_call" | custom-call | flops 1000000000 | bytes 6000000 | tf_op jit(solution)/shard_map/pallas_call | solution.py:557
  36.3 4.8 %all-to-all-start.1 = ((s32[128,1,1280]{2,1,0:T(1,128)}), s32[128,1,1280]{2,1,0:T(1,128)S(1)}, u32[]{:S(2)}, u32[]{:S(2)}) async-start(s32[128,1,1280]{2,1,0:T(1,128)} %bitcast.7), calls=%async_computation.1 | async-start | bytes 1310720 | tf_op jit(solution)/shard_map/all_to_all | solution.py:625
  41.2 11.6 %shard_map.152 = (f32[128,256]{1,0:T(8,128)S(1)}, f32[8,256]{1,0:T(8,128)S(1)}, f32[8,256]{1,0:T(8,128)S(1)}, f32[8,256]{1,0:T(8,128)S(1)}, f32[8,256]{1,0:T(8,128)S(1)}) custom-call(f32[3,4096]{1,0:T(4,128)} %disp.5, f32[3,4096]{1,0:T(4,128)} %direction.5, f32[8,256]{1,0:T(8,128)S(1)} %collective-permute-done.2.p2.p0, ...), custom_call_target="tpu_custom_call" | custom-call | flops 4000000000 | bytes 10000000 | tf_op jit(solution)/shard_map/pallas_call | solution.py:535
  52.7 1.0 %collective-permute-start.4 = (f32[8,256]{1,0:T(8,128)S(1)}, f32[8,256]{1,0:T(8,128)S(1)}, u32[]{:S(2)}, u32[]{:S(2)}) collective-permute-start(f32[8,256]{1,0:T(8,128)S(1)} %get-tuple-element.24), channel_id=1, source_target_pairs={{0,2},{1,3},{2,4},{3,5},{4,6},{5,7},{6,8},{7,9},{8,10},{9,11},{10,... | collective-permute-start | bytes 24584 | tf_op jit(solution)/shard_map/ppermute | solution.py:26
  53.7 0.0 collective-permute-start.5
  53.7 7.2 %collective-permute-start.6 = (f32[8,256]{1,0:T(8,128)S(1)}, f32[8,256]{1,0:T(8,128)S(1)}, u32[]{:S(2)}, u32[]{:S(2)}) collective-permute-start(f32[8,256]{1,0:T(8,128)S(1)} %get-tuple-element.26), channel_id=1, source_target_pairs={{0,127},{1,0},{2,1},{3,2},{4,3},{5,4},{6,5},{7,6},{8,7},{9,8},{10,... | collective-permute-start | bytes 24584 | tf_op jit(solution)/shard_map/ppermute | solution.py:26
  60.9 1.1 %collective-permute-start.7 = (f32[8,256]{1,0:T(8,128)S(1)}, f32[8,256]{1,0:T(8,128)S(1)}, u32[]{:S(2)}, u32[]{:S(2)}) collective-permute-start(f32[8,256]{1,0:T(8,128)S(1)} %get-tuple-element.27), channel_id=1, source_target_pairs={{0,126},{1,127},{2,0},{3,1},{4,2},{5,3},{6,4},{7,5},{8,6},{9,7},{1... | collective-permute-start | bytes 24584 | tf_op jit(solution)/shard_map/ppermute | solution.py:26
  62.0 5.3 %shard_map.153.base = f32[128,256]{1,0:T(8,128)S(1)} custom-call(f32[128,256]{1,0:T(8,128)S(1)} %get-tuple-element.22.own, s32[12,128]{1,0:T(8,128)} %bitcast.15, s32[32,128]{1,0:T(8,128)} %bitcast.13, f32[24,4096]{1,0:T(8,128)S(1)} %get-tuple-element.23.weights, f32[9,36,4096]{2,1,0:T(8,128)} %source.5), custom_call_target="tpu_custom_call" | custom-call | flops 1000000000 | bytes 6000000 | tf_op jit(solution)/shard_map/pallas_call | solution.py:578
  67.3 0.0 collective-permute-done.4.p0
  67.3 0.0 collective-permute-done.5.p1
  67.3 0.0 collective-permute-done.6.p2
  67.3 0.0 collective-permute-done.7.p3
  67.3 0.0 all-to-all-done.1
  67.3 4.2 %shard_map.154 = (f32[3,4096]{1,0:T(4,128)}, f32[3,4096]{1,0:T(4,128)}) custom-call(s32[1280,128]{1,0:T(8,128)S(1)} %bitcast.11, s32[32,128]{1,0:T(8,128)S(1)} %get-tuple-element.21.slots, s32[12,128]{1,0:T(8,128)} %bitcast.18, f32[128,256]{1,0:T(8,128)S(1)} %shard_map.153.base, f32[8,256]{1,0:T(8,128)S(1)} %collective-permute-done.4.p0, ...), custom_call_target="tpu_custom_call" | custom-call | flops 1000000000 | bytes 1000000 | tf_op jit(solution)/shard_map/pallas_call | solution.py:591
Async XLA Ops:
  3.8 26.4 %all-to-all-start = ((s32[128,1,1280]{2,1,0:T(1,128)}), s32[128,1,1280]{2,1,0:T(1,128)S(1)}, u32[]{:S(2)}, u32[]{:S(2)}) async-start(s32[128,1,1280]{2,1,0:T(1,128)} %bitcast.3), calls=%async_computation | async-start | bytes 1310720 | tf_op jit(solution)/shard_map/all_to_all | solution.py:625
  14.9 14.2 %collective-permute-start = (f32[8,256]{1,0:T(8,128)S(1)}, f32[8,256]{1,0:T(8,128)S(1)}, u32[]{:S(2)}, u32[]{:S(2)}) collective-permute-start(f32[8,256]{1,0:T(8,128)S(1)} %get-tuple-element.16), channel_id=1, source_target_pairs={{0,1},{1,2},{2,3},{3,4},{4,5},{5,6},{6,7},{7,8},{8,9},{9,10},{10,1... | collective-permute-start | bytes 24584 | tf_op jit(solution)/shard_map/ppermute | solution.py:26
  15.0 14.7 %collective-permute-start.1 = (f32[8,256]{1,0:T(8,128)S(1)}, f32[8,256]{1,0:T(8,128)S(1)}, u32[]{:S(2)}, u32[]{:S(2)}) collective-permute-start(f32[8,256]{1,0:T(8,128)S(1)} %get-tuple-element.17), channel_id=1, source_target_pairs={{0,2},{1,3},{2,4},{3,5},{4,6},{5,7},{6,8},{7,9},{8,10},{9,11},{10,... | collective-permute-start | bytes 24584 | tf_op jit(solution)/shard_map/ppermute | solution.py:26
  16.2 13.5 %collective-permute-start.2 = (f32[8,256]{1,0:T(8,128)S(1)}, f32[8,256]{1,0:T(8,128)S(1)}, u32[]{:S(2)}, u32[]{:S(2)}) collective-permute-start(f32[8,256]{1,0:T(8,128)S(1)} %get-tuple-element.18), channel_id=1, source_target_pairs={{0,126},{1,127},{2,0},{3,1},{4,2},{5,3},{6,4},{7,5},{8,6},{9,7},{1... | collective-permute-start | bytes 24584 | tf_op jit(solution)/shard_map/ppermute | solution.py:26
  22.6 7.2 %collective-permute-start.3 = (f32[8,256]{1,0:T(8,128)S(1)}, f32[8,256]{1,0:T(8,128)S(1)}, u32[]{:S(2)}, u32[]{:S(2)}) collective-permute-start(f32[8,256]{1,0:T(8,128)S(1)} %get-tuple-element.19), channel_id=1, source_target_pairs={{0,127},{1,0},{2,1},{3,2},{4,3},{5,4},{6,5},{7,6},{8,7},{9,8},{10,... | collective-permute-start | bytes 24584 | tf_op jit(solution)/shard_map/ppermute | solution.py:26
  36.3 31.0 %all-to-all-start.1 = ((s32[128,1,1280]{2,1,0:T(1,128)}), s32[128,1,1280]{2,1,0:T(1,128)S(1)}, u32[]{:S(2)}, u32[]{:S(2)}) async-start(s32[128,1,1280]{2,1,0:T(1,128)} %bitcast.7), calls=%async_computation.1 | async-start | bytes 1310720 | tf_op jit(solution)/shard_map/all_to_all | solution.py:625
  52.7 14.5 %collective-permute-start.4 = (f32[8,256]{1,0:T(8,128)S(1)}, f32[8,256]{1,0:T(8,128)S(1)}, u32[]{:S(2)}, u32[]{:S(2)}) collective-permute-start(f32[8,256]{1,0:T(8,128)S(1)} %get-tuple-element.24), channel_id=1, source_target_pairs={{0,2},{1,3},{2,4},{3,5},{4,6},{5,7},{6,8},{7,9},{8,10},{9,11},{10,... | collective-permute-start | bytes 24584 | tf_op jit(solution)/shard_map/ppermute | solution.py:26
  53.7 13.6 %collective-permute-start.5 = (f32[8,256]{1,0:T(8,128)S(1)}, f32[8,256]{1,0:T(8,128)S(1)}, u32[]{:S(2)}, u32[]{:S(2)}) collective-permute-start(f32[8,256]{1,0:T(8,128)S(1)} %get-tuple-element.25), channel_id=1, source_target_pairs={{0,1},{1,2},{2,3},{3,4},{4,5},{5,6},{6,7},{7,8},{8,9},{9,10},{10,1... | collective-permute-start | bytes 24584 | tf_op jit(solution)/shard_map/ppermute | solution.py:26
  53.7 13.6 %collective-permute-start.6 = (f32[8,256]{1,0:T(8,128)S(1)}, f32[8,256]{1,0:T(8,128)S(1)}, u32[]{:S(2)}, u32[]{:S(2)}) collective-permute-start(f32[8,256]{1,0:T(8,128)S(1)} %get-tuple-element.26), channel_id=1, source_target_pairs={{0,127},{1,0},{2,1},{3,2},{4,3},{5,4},{6,5},{7,6},{8,7},{9,8},{10,... | collective-permute-start | bytes 24584 | tf_op jit(solution)/shard_map/ppermute | solution.py:26
  60.9 6.4 %collective-permute-start.7 = (f32[8,256]{1,0:T(8,128)S(1)}, f32[8,256]{1,0:T(8,128)S(1)}, u32[]{:S(2)}, u32[]{:S(2)}) collective-permute-start(f32[8,256]{1,0:T(8,128)S(1)} %get-tuple-element.27), channel_id=1, source_target_pairs={{0,126},{1,127},{2,0},{3,1},{4,2},{5,3},{6,4},{7,5},{8,6},{9,7},{1... | collective-permute-start | bytes 24584 | tf_op jit(solution)/shard_map/ppermute | solution.py:26

commit v4 on v3

--- a/solution.py
+++ b/solution.py
@@ -255,7 +255,7 @@
     put_tails(out, tails, 32)
 
 
-def element_kernel(disp, direction, p0, p1, p2, p3, nodes, blocks, own, s0, s1, s2, s3, table, hits, x, y, held, sums, sems):
+def element_kernel(fields, p0, p1, p2, p3, nodes, blocks, own, s0, s1, s2, s3, hits, x, y, held, sums, sems):
     chunk = blocks.shape[0] // sems.shape[0]
     copies = [
         pltpu.make_async_copy(
@@ -265,10 +265,8 @@
     ]
     for copy in copies:
         copy.start()
-    fill_table(table, disp, direction)
-    for o, piece in enumerate((p0, p1, p2, p3)):
-        table[8 * (16 + o) : 8 * (17 + o), :] = piece[...]
-    coarse = table[...].astype(BF16)
+    pieces = [piece[...] for piece in (p0, p1, p2, p3)]
+    coarse = jnp.concatenate([fields[...]] + pieces, 0).astype(BF16)
     elements = nodes.shape[1]
 
     def gather_node(a, carry):
@@ -285,7 +283,7 @@
                 ]
         return carry
 
-    lax.fori_loop(0, 32, gather_node, 0, unroll=8)
+    lax.fori_loop(0, 32, gather_node, 0, unroll=16)
     y[:, 192:256, :] = jnp.zeros((y.shape[0], 64, LANES), F32)
     for n, copy in enumerate(copies):
         copy.wait()
@@ -323,7 +321,7 @@
             sums[...] += across(wide, hits[:, pl.ds(at, WIDE)])
         return carry
 
-    lax.fori_loop(0, 32, scatter_node, 0, unroll=8)
+    lax.fori_loop(0, 32, scatter_node, 0, unroll=16)
     for g in range(16):
         own[8 * g : 8 * g + 8, :] = sums[16 * g : 16 * g + 8, :] + sums[16 * g + 8 : 16 * g + 16, :]
     for o, piece in enumerate((s0, s1, s2, s3)):
@@ -354,9 +352,8 @@
         lax.fori_loop(0, part, step, 0, unroll=True)
 
 
-def near_kernel(disp, direction, nodes, pair, gap, source, out, table, faces, fields, mortar, sems):
+def near_kernel(table, nodes, pair, gap, source, out, faces, fields, mortar, sems):
     copies = fetch(source, mortar, sems)
-    fill_table(table, disp, direction)
     fill_faces(faces, cut(table[...]), nodes)
     left = jnp.concatenate(cut(jnp.concatenate(padded_fields(faces), 0)), 0)
     groups = out.shape[1] // LANES
@@ -428,8 +425,9 @@
         at = pl.ds(lane, LANES)
         force = jnp.concatenate(adjoint(mortar, lane, weights[:, at]), 0)
         forces[:, at] = jnp.concatenate(cut(force), 0)
-        hits[:, at] = indicator(pair[pl.ds(g, 1), :], LANES)
-
+
+    for g in range(groups):
+        hits[:, LANES * g : LANES * g + LANES] = indicator(pair[g : g + 1, :], LANES)
     over_groups(copies, groups, group)
     sums = across(forces[...], hits[...])
     for g, rows in enumerate(merge(face_sums(sums, faces, nodes), 16)):
@@ -490,9 +488,13 @@
     piece = shape((8, halo_send.shape[1]))
     return call(
         pack_kernel,
-        [piece] * 4 + [shape((WORDS * send.shape[1], LANES), I32), shape((groups, LANES), I32)],
+        [piece] * 4
+        + [
+            shape((WORDS * send.shape[1], LANES), I32),
+            shape((groups, LANES), I32),
+            shape((128, WIDE)),
+        ],
         [
-            pltpu.VMEM((128, WIDE), F32),
             pltpu.VMEM((96, LANES), F32),
             pltpu.VMEM((LANES, LANES), I32),
             pltpu.VMEM((8 * groups, LANES), I32),
@@ -512,31 +514,26 @@
     return [pltpu.VMEM(mortar.shape, F32), pltpu.SemaphoreType.DMA((stretches,))]
 
 
-def near_part(disp, direction, slaves, pair, mortar, gap):
+def near_part(table, slaves, pair, mortar, gap):
     pairs = mortar.shape[2]
     return call(
         near_kernel,
         shape((24, pairs)),
-        [
-            pltpu.VMEM((128, WIDE), F32),
-            pltpu.VMEM((96, LANES), F32),
-            pltpu.VMEM((80, pairs), F32),
-        ]
+        [pltpu.VMEM((96, LANES), F32), pltpu.VMEM((80, pairs), F32)]
         + mortar_scratch(mortar, 8),
         10**9,
         6 * 10**6,
         14,
-        in_specs=inputs(5),
-    )(*settled(disp, direction, slaves, pair, gap, mortar))
-
-
-def elements_part(disp, direction, pieces, nodes, blocks):
+        in_specs=inputs(4),
+    )(table, *settled(slaves, pair, gap, mortar))
+
+
+def elements_part(table, pieces, nodes, blocks):
     elements = nodes.shape[1]
     return call(
         element_kernel,
         [shape((128, WIDE))] + [shape((8, WIDE))] * 4,
         [
-            pltpu.VMEM((160, WIDE), F32),
             pltpu.VMEM((WIDE, 32 * elements), BF16),
             pltpu.VMEM((elements // LANES, 256, LANES), F32),
             pltpu.VMEM((elements // LANES, 256, LANES), F32),
@@ -547,8 +544,8 @@
         4 * 10**9,
         10**7,
         32,
-        in_specs=inputs(7),
-    )(*settled(disp, direction), *pieces, *settled(nodes, blocks))
+        in_specs=inputs(6),
+    )(table, *pieces, *settled(nodes, blocks))
 
 
 def far_part(arrived, near, mortar, pieces):
@@ -626,12 +623,12 @@
         return value.reshape(WORDS * peers, LANES)
 
     packed = pack(disp, direction, halo_send, masters, send, mortar_count)
-    outgoing, words, slots = packed[:4], packed[4], packed[5]
+    outgoing, words, slots, table = packed[:4], packed[4], packed[5], packed[6]
     arrived = exchange(words)
     received = {o: shifted(outgoing[o], "dom", moves[o]) for o in (2, 3, 0, 1)}
     pieces = [received[o] for o in range(4)]
-    near = near_part(disp, direction, slaves, pair, slave_mortar, gap_offset)
-    element = elements_part(disp, direction, pieces, elem_nodes, blocks)
+    near = near_part(table, slaves, pair, slave_mortar, gap_offset)
+    element = elements_part(table, pieces, elem_nodes, blocks)
     own, sums = element[0], element[1:]
     shared = [shifted(sums[o], "dom", -moves[o]) for o in range(4)]
     back, weights = far_part(arrived, near, master_mortar, pieces)

time: 72 us -> 71.4 us (level)
  transfers between devices with their start and end apart: 10 -> 10, of which waited for: 3 -> 3; matrix products, arithmetic and copies ran while one was open for 0% -> 0% of each run, Pallas kernels for 29% -> 28%
where the time goes in v4:
time: 71.4 us; the launch traced here: 70.9 us
  starting transfers between devices  34.1 us (48%)
  Pallas kernels  33.6 us (47%)
  waiting for transfers between devices  2.51 us (4%)
  between operations  0.73 us (1%)
    ppermute x8, starting transfers between devices, shifted(): return lax.ppermute(value, axis, pairs)  18.1 us
    all_to_all x2, starting transfers between devices, exchange(): lax.all_to_all(value, 'dom', split_axis=0, concat_axis=0, tiled=True)  16 us
    pallas_call x1, Pallas kernels, elements_part(): call(element_kernel, [shape((128, WIDE))] + [shape((8, WIDE))] * 4, [pltp...  11 us
    pallas_call x1, Pallas kernels, far_part(): call(far_kernel, [shape(arrived.shape, I32), shape((24, pairs))], [tails,...  6.11 us
    pallas_call x1, Pallas kernels, slave_part(): call(slave_kernel, shape((128, WIDE)), sum_scratch(pairs) + mortar_scratc...  5.24 us
    pallas_call x1, Pallas kernels, last_part(): call(last_kernel, [shape(load.shape), shape(load.shape)], [pltpu.VMEM((8...  4.21 us
    pallas_call x1, Pallas kernels, near_part(): call(near_kernel, shape((24, pairs)), [pltpu.VMEM((96, LANES), F32), pltp...  3.94 us
    pallas_call x1, Pallas kernels, pack(): call(pack_kernel, [piece] * 4 + [shape((WORDS * send.shape[1], LANES), I3...  3.16 us
  transfers between devices with their start and end apart: 10, of which 3 were waited for; matrix products, arithmetic and copies ran while one was open for 0% of the time, Pallas kernels for 28%

profile of v4, /device:TPU:0, one launch (start us, length us, event | category | flops | bytes accessed | tf_op | source)
XLA Modules:
  0.0 70.9 jit_solution(5055688509670586177)
XLA Ops:
  0.6 3.2 %shard_map.149 = (f32[8,256]{1,0:T(8,128)S(1)}, f32[8,256]{1,0:T(8,128)S(1)}, f32[8,256]{1,0:T(8,128)S(1)}, f32[8,256]{1,0:T(8,128)S(1)}, s32[1280,128]{1,0:T(8,...) custom-call(f32[3,4096]{1,0:T(4,128)} %disp.1, f32[3,4096]{1,0:T(4,128)} %direction.1, s32[4,256]{1,0:T(4,128)} %halo.3, ...), custom_call_target="tpu_custom_call" | custom-call | flops 1000000000 | bytes 1000000 | tf_op jit(solution)/shard_map/pallas_call | solution.py:489
  3.8 11.1 %all-to-all-start = ((s32[128,1,1280]{2,1,0:T(1,128)}), s32[128,1,1280]{2,1,0:T(1,128)S(1)}, u32[]{:S(2)}, u32[]{:S(2)}) async-start(s32[128,1,1280]{2,1,0:T(1,128)} %bitcast.3), calls=%async_computation | async-start | bytes 1310720 | tf_op jit(solution)/shard_map/all_to_all | solution.py:622
  14.9 0.1 collective-permute-start
  15.0 1.2 %collective-permute-start.1 = (f32[8,256]{1,0:T(8,128)S(1)}, f32[8,256]{1,0:T(8,128)S(1)}, u32[]{:S(2)}, u32[]{:S(2)}) collective-permute-start(f32[8,256]{1,0:T(8,128)S(1)} %get-tuple-element.19), channel_id=1, source_target_pairs={{0,2},{1,3},{2,4},{3,5},{4,6},{5,7},{6,8},{7,9},{8,10},{9,11},{10,... | collective-permute-start | bytes 24584 | tf_op jit(solution)/shard_map/ppermute | solution.py:26
  16.2 6.3 %collective-permute-start.2 = (f32[8,256]{1,0:T(8,128)S(1)}, f32[8,256]{1,0:T(8,128)S(1)}, u32[]{:S(2)}, u32[]{:S(2)}) collective-permute-start(f32[8,256]{1,0:T(8,128)S(1)} %get-tuple-element.20), channel_id=1, source_target_pairs={{0,126},{1,127},{2,0},{3,1},{4,2},{5,3},{6,4},{7,5},{8,6},{9,7},{1... | collective-permute-start | bytes 24584 | tf_op jit(solution)/shard_map/ppermute | solution.py:26
  22.5 1.2 %collective-permute-start.3 = (f32[8,256]{1,0:T(8,128)S(1)}, f32[8,256]{1,0:T(8,128)S(1)}, u32[]{:S(2)}, u32[]{:S(2)}) collective-permute-start(f32[8,256]{1,0:T(8,128)S(1)} %get-tuple-element.21), channel_id=1, source_target_pairs={{0,127},{1,0},{2,1},{3,2},{4,3},{5,4},{6,5},{7,6},{8,7},{9,8},{10,... | collective-permute-start | bytes 24584 | tf_op jit(solution)/shard_map/ppermute | solution.py:26
  23.8 3.9 %shard_map.150.near = f32[24,4096]{1,0:T(8,128)S(1)} custom-call(f32[128,256]{1,0:T(8,128)S(1)} %get-tuple-element.17.table.fields, s32[12,128]{1,0:T(8,128)} %bitcast.14, s32[32,128]{1,0:T(8,128)} %bitcast.12, f32[9,4096]{1,0:T(8,128)} %gap.1, f32[9,36,4096]{2,1,0:T(8,128)} %source.5), custom_call_target="tpu_custom_call" | custom-call | flops 1000000000 | bytes 6000000 | tf_op jit(solution)/shard_map/pallas_call | solution.py:519
  27.7 1.4 %collective-permute-done.p0.p2 = f32[8,256]{1,0:T(8,128)S(1)} collective-permute-done((f32[8,256]{1,0:T(8,128)S(1)}, f32[8,256]{1,0:T(8,128)S(1)}, u32[]{:S(2)}, u32[]{:S(2)}) %collective-permute-start) | collective-permute-done | bytes 8224 | tf_op jit(solution)/shard_map/ppermute | solution.py:26
  29.2 0.5 collective-permute-done.1.p1.p3
  29.7 0.0 collective-permute-done.2.p2.p0
  29.7 0.0 collective-permute-done.3.p3.p1
  29.7 0.5 all-to-all-done
  30.2 6.1 %shard_map.151 = (s32[1280,128]{1,0:T(8,128)}, f32[24,4096]{1,0:T(8,128)S(1)}) custom-call(s32[1280,128]{1,0:T(8,128)S(1)} %bitcast.10, f32[24,4096]{1,0:T(8,128)S(1)} %shard_map.150.near, f32[8,256]{1,0:T(8,128)S(1)} %collective-permute-done.p0.p2, f32[8,256]{1,0:T(8,128)S(1)} %collective-permute-done.1.p1.p3, f32[8,256]{1,0:T(8,128)S(1)} %collective-permute-done.2.p2.p0, ...), custom_call_target="tpu_custom_call" | custom-call | flops 1000000000 | bytes 6000000 | tf_op jit(solution)/shard_map/pallas_call | solution.py:554
  36.3 4.8 %all-to-all-start.1 = ((s32[128,1,1280]{2,1,0:T(1,128)}), s32[128,1,1280]{2,1,0:T(1,128)S(1)}, u32[]{:S(2)}, u32[]{:S(2)}) async-start(s32[128,1,1280]{2,1,0:T(1,128)} %bitcast.7), calls=%async_computation.1 | async-start | bytes 1310720 | tf_op jit(solution)/shard_map/all_to_all | solution.py:622
  41.2 11.0 %shard_map.152 = (f32[128,256]{1,0:T(8,128)S(1)}, f32[8,256]{1,0:T(8,128)S(1)}, f32[8,256]{1,0:T(8,128)S(1)}, f32[8,256]{1,0:T(8,128)S(1)}, f32[8,256]{1,0:T(8,128)S(1)}) custom-call(f32[128,256]{1,0:T(8,128)S(1)} %get-tuple-element.17.table.fields, f32[8,256]{1,0:T(8,128)S(1)} %collective-permute-done.2.p2.p0, f32[8,256]{1,0:T(8,128)S(1)} %collective-permute-done.3.p3.p1, ...), custom_call_target="tpu_custom_call" | custom-call | flops 4000000000 | bytes 10000000 | tf_op jit(solution)/shard_map/pallas_call | solution.py:533
  52.1 1.0 %collective-permute-start.4 = (f32[8,256]{1,0:T(8,128)S(1)}, f32[8,256]{1,0:T(8,128)S(1)}, u32[]{:S(2)}, u32[]{:S(2)}) collective-permute-start(f32[8,256]{1,0:T(8,128)S(1)} %get-tuple-element.26), channel_id=1, source_target_pairs={{0,2},{1,3},{2,4},{3,5},{4,6},{5,7},{6,8},{7,9},{8,10},{9,11},{10,... | collective-permute-start | bytes 24584 | tf_op jit(solution)/shard_map/ppermute | solution.py:26
  53.1 0.0 collective-permute-start.5
  53.1 7.2 %collective-permute-start.6 = (f32[8,256]{1,0:T(8,128)S(1)}, f32[8,256]{1,0:T(8,128)S(1)}, u32[]{:S(2)}, u32[]{:S(2)}) collective-permute-start(f32[8,256]{1,0:T(8,128)S(1)} %get-tuple-element.28), channel_id=1, source_target_pairs={{0,127},{1,0},{2,1},{3,2},{4,3},{5,4},{6,5},{7,6},{8,7},{9,8},{10,... | collective-permute-start | bytes 24584 | tf_op jit(solution)/shard_map/ppermute | solution.py:26
  60.3 1.1 %collective-permute-start.7 = (f32[8,256]{1,0:T(8,128)S(1)}, f32[8,256]{1,0:T(8,128)S(1)}, u32[]{:S(2)}, u32[]{:S(2)}) collective-permute-start(f32[8,256]{1,0:T(8,128)S(1)} %get-tuple-element.29), channel_id=1, source_target_pairs={{0,126},{1,127},{2,0},{3,1},{4,2},{5,3},{6,4},{7,5},{8,6},{9,7},{1... | collective-permute-start | bytes 24584 | tf_op jit(solution)/shard_map/ppermute | solution.py:26
  61.4 5.2 %shard_map.153.base = f32[128,256]{1,0:T(8,128)S(1)} custom-call(f32[128,256]{1,0:T(8,128)S(1)} %get-tuple-element.24.own, s32[12,128]{1,0:T(8,128)} %bitcast.15, s32[32,128]{1,0:T(8,128)} %bitcast.13, f32[24,4096]{1,0:T(8,128)S(1)} %get-tuple-element.25.weights, f32[9,36,4096]{2,1,0:T(8,128)} %source.5), custom_call_target="tpu_custom_call" | custom-call | flops 1000000000 | bytes 6000000 | tf_op jit(solution)/shard_map/pallas_call | solution.py:575
  66.7 0.0 collective-permute-done.4.p0
  66.7 0.0 collective-permute-done.5.p1
  66.7 0.0 collective-permute-done.6.p2
  66.7 0.0 collective-permute-done.7.p3
  66.7 0.0 all-to-all-done.1
  66.7 4.2 %shard_map.154 = (f32[3,4096]{1,0:T(4,128)}, f32[3,4096]{1,0:T(4,128)}) custom-call(s32[1280,128]{1,0:T(8,128)S(1)} %bitcast.11, s32[32,128]{1,0:T(8,128)S(1)} %get-tuple-element.23.slots, s32[12,128]{1,0:T(8,128)} %bitcast.18, f32[128,256]{1,0:T(8,128)S(1)} %shard_map.153.base, f32[8,256]{1,0:T(8,128)S(1)} %collective-permute-done.4.p0, ...), custom_call_target="tpu_custom_call" | custom-call | flops 1000000000 | bytes 1000000 | tf_op jit(solution)/shard_map/pallas_call | solution.py:588
Async XLA Ops:
  3.8 26.4 %all-to-all-start = ((s32[128,1,1280]{2,1,0:T(1,128)}), s32[128,1,1280]{2,1,0:T(1,128)S(1)}, u32[]{:S(2)}, u32[]{:S(2)}) async-start(s32[128,1,1280]{2,1,0:T(1,128)} %bitcast.3), calls=%async_computation | async-start | bytes 1310720 | tf_op jit(solution)/shard_map/all_to_all | solution.py:622
  14.9 14.2 %collective-permute-start = (f32[8,256]{1,0:T(8,128)S(1)}, f32[8,256]{1,0:T(8,128)S(1)}, u32[]{:S(2)}, u32[]{:S(2)}) collective-permute-start(f32[8,256]{1,0:T(8,128)S(1)} %get-tuple-element.18), channel_id=1, source_target_pairs={{0,1},{1,2},{2,3},{3,4},{4,5},{5,6},{6,7},{7,8},{8,9},{9,10},{10,1... | collective-permute-start | bytes 24584 | tf_op jit(solution)/shard_map/ppermute | solution.py:26
  15.0 14.7 %collective-permute-start.1 = (f32[8,256]{1,0:T(8,128)S(1)}, f32[8,256]{1,0:T(8,128)S(1)}, u32[]{:S(2)}, u32[]{:S(2)}) collective-permute-start(f32[8,256]{1,0:T(8,128)S(1)} %get-tuple-element.19), channel_id=1, source_target_pairs={{0,2},{1,3},{2,4},{3,5},{4,6},{5,7},{6,8},{7,9},{8,10},{9,11},{10,... | collective-permute-start | bytes 24584 | tf_op jit(solution)/shard_map/ppermute | solution.py:26
  16.2 13.5 %collective-permute-start.2 = (f32[8,256]{1,0:T(8,128)S(1)}, f32[8,256]{1,0:T(8,128)S(1)}, u32[]{:S(2)}, u32[]{:S(2)}) collective-permute-start(f32[8,256]{1,0:T(8,128)S(1)} %get-tuple-element.20), channel_id=1, source_target_pairs={{0,126},{1,127},{2,0},{3,1},{4,2},{5,3},{6,4},{7,5},{8,6},{9,7},{1... | collective-permute-start | bytes 24584 | tf_op jit(solution)/shard_map/ppermute | solution.py:26
  22.5 7.2 %collective-permute-start.3 = (f32[8,256]{1,0:T(8,128)S(1)}, f32[8,256]{1,0:T(8,128)S(1)}, u32[]{:S(2)}, u32[]{:S(2)}) collective-permute-start(f32[8,256]{1,0:T(8,128)S(1)} %get-tuple-element.21), channel_id=1, source_target_pairs={{0,127},{1,0},{2,1},{3,2},{4,3},{5,4},{6,5},{7,6},{8,7},{9,8},{10,... | collective-permute-start | bytes 24584 | tf_op jit(solution)/shard_map/ppermute | solution.py:26
  36.3 30.4 %all-to-all-start.1 = ((s32[128,1,1280]{2,1,0:T(1,128)}), s32[128,1,1280]{2,1,0:T(1,128)S(1)}, u32[]{:S(2)}, u32[]{:S(2)}) async-start(s32[128,1,1280]{2,1,0:T(1,128)} %bitcast.7), calls=%async_computation.1 | async-start | bytes 1310720 | tf_op jit(solution)/shard_map/all_to_all | solution.py:622
  52.1 14.5 %collective-permute-start.4 = (f32[8,256]{1,0:T(8,128)S(1)}, f32[8,256]{1,0:T(8,128)S(1)}, u32[]{:S(2)}, u32[]{:S(2)}) collective-permute-start(f32[8,256]{1,0:T(8,128)S(1)} %get-tuple-element.26), channel_id=1, source_target_pairs={{0,2},{1,3},{2,4},{3,5},{4,6},{5,7},{6,8},{7,9},{8,10},{9,11},{10,... | collective-permute-start | bytes 24584 | tf_op jit(solution)/shard_map/ppermute | solution.py:26
  53.1 13.6 %collective-permute-start.5 = (f32[8,256]{1,0:T(8,128)S(1)}, f32[8,256]{1,0:T(8,128)S(1)}, u32[]{:S(2)}, u32[]{:S(2)}) collective-permute-start(f32[8,256]{1,0:T(8,128)S(1)} %get-tuple-element.27), channel_id=1, source_target_pairs={{0,1},{1,2},{2,3},{3,4},{4,5},{5,6},{6,7},{7,8},{8,9},{9,10},{10,1... | collective-permute-start | bytes 24584 | tf_op jit(solution)/shard_map/ppermute | solution.py:26
  53.1 13.6 %collective-permute-start.6 = (f32[8,256]{1,0:T(8,128)S(1)}, f32[8,256]{1,0:T(8,128)S(1)}, u32[]{:S(2)}, u32[]{:S(2)}) collective-permute-start(f32[8,256]{1,0:T(8,128)S(1)} %get-tuple-element.28), channel_id=1, source_target_pairs={{0,127},{1,0},{2,1},{3,2},{4,3},{5,4},{6,5},{7,6},{8,7},{9,8},{10,... | collective-permute-start | bytes 24584 | tf_op jit(solution)/shard_map/ppermute | solution.py:26
  60.3 6.4 %collective-permute-start.7 = (f32[8,256]{1,0:T(8,128)S(1)}, f32[8,256]{1,0:T(8,128)S(1)}, u32[]{:S(2)}, u32[]{:S(2)}) collective-permute-start(f32[8,256]{1,0:T(8,128)S(1)} %get-tuple-element.29), channel_id=1, source_target_pairs={{0,126},{1,127},{2,0},{3,1},{4,2},{5,3},{6,4},{7,5},{8,6},{9,7},{1... | collective-permute-start | bytes 24584 | tf_op jit(solution)/shard_map/ppermute | solution.py:26
